TPU v7x, 128 devices: a whole 4x4x4 slice. The times are simulated.
128 devices in a mesh: band: 16 (over z_lo, x, core), pw: 8 (over z_hi, y).
Axes of the slice: x: 4, y: 4, z: 4 (z_hi: 2, z_lo: 2; z = z_hi * 2 + z_lo), core: 2. Of those that a mesh axis runs over, the one named last changes fastest.
Arguments:
- wave_coeffs: bfloat16 [16, 2, 491520], P('band', None, 'pw'), may hold values from -6 to 6
- potential: float32 [96, 9216], P(None, 'pw'), may hold values from -1.5 to 3
- sphere_index: int32 [491520], P('pw'), may hold values from 0 to 884735, as said below
- rotation: float32 [16, 64], P('pw'), may hold values from -1.5 to 1.5
- panel_order: int32 [16], replicated, may hold values from 0 to 15, each once
Outputs:
- rotated: float32 [64, 2, 491520], P('band', None, 'pw')
Inputs may be any that keep to these rules, and one draw needn't show every extreme that they name: `sphere_index`: all entries are distinct. The k-th run of 61440 entries is increasing and lies in the grid planes x = k * 12 to (k + 1) * 12 - 1, and holds the first and the last cell of those planes.
All inputs are finite; a program needn't handle non-finite values.
Results may differ from a plain program's by a relative error of at most 0.0003.
Values sent between devices are 32-bit elements; how exact they have to be, the bound alone decides.
A program may use at most 192 MiB of HBM per device.

v0:
```python
import math

import jax
import jax.numpy as jnp
from jax import lax
from jax.sharding import PartitionSpec as P

NG = 96


HIGHEST = lax.Precision.HIGHEST


def broadcast(block, axis, source):
    block = jnp.where(lax.axis_index(axis) == source, block, jnp.zeros_like(block))
    return lax.psum(block, axis)


def dft_tables(length, direction):
    counter = jnp.arange(length, dtype=jnp.int32)
    products = counter[:, None] * counter[None, :] % length
    angles = 2.0 * math.pi / length * products.astype(jnp.float32)
    scaling = 1.0 / math.sqrt(length)
    cosines = jnp.cos(angles) * scaling
    sine_table = direction * jnp.sin(angles) * scaling
    upper = jnp.stack([cosines, -sine_table], axis=1)
    lower = jnp.stack([sine_table, cosines], axis=1)
    return jnp.stack([upper, lower], axis=0)


def along_axis(field, table, pattern):
    return jnp.einsum(pattern, table, field, precision=HIGHEST)


def signed_frequency(position):
    return jnp.where(position < NG // 2, position, position - NG).astype(jnp.float32)


def kinetic(sphere_index):
    plane_cells = NG * NG
    index_x = sphere_index // plane_cells
    index_y = sphere_index // NG % NG
    index_z = sphere_index % NG
    total = (
        signed_frequency(index_x) ** 2
        + signed_frequency(index_y) ** 2
        + signed_frequency(index_z) ** 2
    )
    return 2.0 * total / float((NG // 2) ** 2)


def shards(wave_coeffs, potential, sphere_index, rotation, panel_order):
    groups = lax.axis_size("pw")
    band_count = wave_coeffs.shape[0]
    slab_planes = NG // groups
    slab_cells = slab_planes * NG * NG
    local_index = sphere_index % slab_cells
    values = wave_coeffs.astype(jnp.float32)
    kinetic_term = kinetic(sphere_index)
    inverse = dft_tables(NG, 1.0)
    forward = dft_tables(NG, -1.0)
    scattered = (
        jnp.zeros((band_count, 2, slab_cells), jnp.float32).at[:, :, local_index].set(values)
    )
    field = scattered.reshape(band_count, 2, slab_planes, NG, NG)
    field = along_axis(field, inverse, "okcn,bcxyn->boxyk")
    field = along_axis(field, inverse, "okcn,bcxnz->boxkz")
    local_field = potential.reshape(NG, NG // groups, NG)
    lines = along_axis(
        lax.all_to_all(field, "pw", split_axis=3, concat_axis=2, tiled=True),
        inverse,
        "okcn,bcnyz->bokyz",
    )
    lines = local_field[None, None] * lines
    lines = along_axis(lines, forward, "okcn,bcnyz->bokyz")
    planes = lax.all_to_all(lines, "pw", split_axis=2, concat_axis=3, tiled=True)
    planes = along_axis(planes, forward, "okcn,bcxnz->boxkz")
    planes = along_axis(planes, forward, "okcn,bcxyn->boxyk")
    back = planes.reshape(band_count, 2, slab_cells)[:, :, local_index]
    applied = kinetic_term[None, None] * values + back
    panel_rows = rotation.shape[0] // 2
    panel_total = 2 * groups

    def receive(panel_turn, assembled):
        wanted = panel_order[panel_turn]
        own_piece = lax.dynamic_slice_in_dim(rotation, wanted % 2 * panel_rows, panel_rows, 0)
        arrived = broadcast(own_piece, "pw", wanted // 2)
        return lax.dynamic_update_slice_in_dim(assembled, arrived, panel_turn * panel_rows, 0)

    ordered = lax.fori_loop(
        0,
        panel_total,
        receive,
        jnp.zeros((panel_rows * panel_total, rotation.shape[1]), jnp.float32),
    )
    regrouped = lax.all_to_all(applied, "band", split_axis=2, concat_axis=0, tiled=True)
    combined = jnp.einsum("ij,icg->jcg", ordered, regrouped, precision=HIGHEST)
    result = lax.all_to_all(combined, "band", split_axis=0, concat_axis=2, tiled=True)
    return result


def solution(mesh):
    return jax.shard_map(
        shards,
        mesh=mesh,
        in_specs=(P("band", None, "pw"), P(None, "pw"), P("pw"), P("pw", None), P()),
        out_specs=P("band", None, "pw"),
        check_vma=False,
    )
```

profile of v0, /device:TPU:1, one launch (start us, length us, event | category | flops | bytes accessed | tf_op | source)
XLA Modules:
  0.0 1376.7 jit_solution(18121275069063612301)
XLA Ops:
  17.9 172.4 %scatter_custom_fusion = f32[2,110592]{0,1:T(8,128)} fusion(s32[61440]{0:T(1024)S(1)} %get-tuple-element.128, f32[61440,2]{1,0:T(8,128)} %copy.49, f32[]{:T(128)} %constant.157.clone.1), kind=kCustom, calls=%fused_computation.3 | custom fusion | bytes 885248 | tf_op jit(solution)/shard_map/scatter | solution.py:63
  190.3 31.1 %copy.67 = f32[2,12,96,96,1]{3,2,0,4,1:T(8,128)S(1)} copy(f32[2,12,96,96,1]{0,3,2,1,4:T(8,128)} %bitcast.123) | data formatting | bytes 1769472 | tf_op jit(solution)/shard_map/reshape.4
  234.6 18.5 %all-to-all-done = f32[1,2,12,96,96]{4,1,2,0,3:T(2,128)S(1)} async-done(((f32[1,2,12,96,96]{4,1,2,0,3:T(2,128)}), f32[1,2,12,96,96]{4,1,2,0,3:T(2,128)S(1)}, u32[]{:S(2)}, u32[]{:S(2)}) %all-to-all-start) | async-done | bytes 884768 | tf_op jit(solution)/shard_map/all_to_all | solution.py:70
  263.1 18.1 %all-to-all-done.1 = f32[1,2,96,12,96]{4,1,3,0,2:T(2,128)S(1)} async-done(((f32[1,2,96,12,96]{4,1,3,0,2:T(2,128)}), f32[1,2,96,12,96]{4,1,3,0,2:T(2,128)S(1)}, u32[]{:S(2)}, u32[]{:S(2)}) %all-to-all-start.1) | async-done | bytes 884768 | tf_op jit(solution)/shard_map/all_to_all | solution.py:76
  285.4 26.6 %copy.89 = f32[1,2,12,96,96]{1,4,3,2,0:T(8,128)} copy(f32[1,2,12,96,96]{4,3,1,2,0:T(8,128)S(1)} %convolution_bitcast_fusion) | data formatting | bytes 1769472 | tf_op jit(solution)/shard_map/reshape | solution.py:79
  312.0 219.8 %gather_fusion = f32[61440,2]{1,0:T(8,128)} fusion(f32[2,110592]{0,1:T(8,128)} %bitcast.126, s32[61440]{0:T(1024)S(1)} %get-tuple-element.127), kind=kCustom, calls=%fused_computation | custom fusion | bytes 1228800 | tf_op jit(solution)/shard_map/gather | solution.py:79
  531.7 16.5 %copy.62 = f32[61440,2]{0,1:T(2,128)S(1)} copy(f32[61440,2]{1,0:T(8,128)} %gather_fusion) | data formatting | bytes 983040 | tf_op jit(solution)/shard_map/gather | solution.py:79
  548.6 43.8 %copy.63 = f32[1,2,61440]{1,0,2:T(1,128)} copy(f32[1,2,61440]{2,1,0:T(2,128)S(1)} %fusion.6) | data formatting | bytes 983040 | tf_op jit(solution)/shard_map/add | solution.py:80
  593.0 272.9 %reduce = f32[61440,2]{1,0:T(8,128)} reduce(f32[61440,1,2]{2,1,0:T(1,128)} %bitcast.124, f32[]{:T(128)} %broadcast.238), dimensions={1}, to_apply=%bitcast.115.reduce_sub_computation | reduce | bytes 983044
  865.8 25.7 %reshape.169 = f32[16,1,7680]{2,1,0:T(1,128)} reshape(f32[61440,2]{1,0:T(8,128)} %reduce) | data formatting | bytes 983040
  897.1 307.6 %while.15 = (s32[]{:T(128)}, f32[16,64]{1,0:T(8,128)S(1)}, s32[16]{0:T(128)S(1)}, f32[2,64]{1,0:T(2,128)S(1)}, s32[]{:T(128)}, /*index=5*/u32[]{:T(128)}, s32[]{:T(128)}, s32[]{:T(128)}, s32[]{:T(128)}) while((s32[]{:T(128)}, f32[16,64]{1,0:T(8,128)S(1)}, s32[16]{0:T(128)S(1)}, f32[2,64]{1,0:T(2,128)S(1)}, s32[]{:T(128)}, ...), condition=%wide.region_2.3_spmd, body=%wide.region_0.2_spmd.sunk | while | flops 155 | bytes 1908 | solution.py:90
  900.0 17.2 %psum.15 = f32[1,64]{1,0:T(1,128)S(1)} all-reduce(f32[1,64]{1,0:T(1,128)S(1)} %broadcast_select_fusion.2), channel_id=1, replica_groups=mesh['band'=16,'pw'=8] {'pw'}, use_global_device_ids=true, to_apply=%region_1.1 | all-reduce | flops 64 | bytes 512 | tf_op jit(solution)/shard_map/while/body/eval_jaxpr/psum | solution.py:16
  920.2 15.7 %psum.15 = f32[1,64]{1,0:T(1,128)S(1)} all-reduce(f32[1,64]{1,0:T(1,128)S(1)} %broadcast_select_fusion.2), channel_id=1, replica_groups=mesh['band'=16,'pw'=8] {'pw'}, use_global_device_ids=true, to_apply=%region_1.1 | all-reduce | flops 64 | bytes 512 | tf_op jit(solution)/shard_map/while/body/eval_jaxpr/psum | solution.py:16
  938.7 16.8 %psum.15 = f32[1,64]{1,0:T(1,128)S(1)} all-reduce(f32[1,64]{1,0:T(1,128)S(1)} %broadcast_select_fusion.2), channel_id=1, replica_groups=mesh['band'=16,'pw'=8] {'pw'}, use_global_device_ids=true, to_apply=%region_1.1 | all-reduce | flops 64 | bytes 512 | tf_op jit(solution)/shard_map/while/body/eval_jaxpr/psum | solution.py:16
  958.4 15.8 %psum.15 = f32[1,64]{1,0:T(1,128)S(1)} all-reduce(f32[1,64]{1,0:T(1,128)S(1)} %broadcast_select_fusion.2), channel_id=1, replica_groups=mesh['band'=16,'pw'=8] {'pw'}, use_global_device_ids=true, to_apply=%region_1.1 | all-reduce | flops 64 | bytes 512 | tf_op jit(solution)/shard_map/while/body/eval_jaxpr/psum | solution.py:16
  977.1 16.9 %psum.15 = f32[1,64]{1,0:T(1,128)S(1)} all-reduce(f32[1,64]{1,0:T(1,128)S(1)} %broadcast_select_fusion.2), channel_id=1, replica_groups=mesh['band'=16,'pw'=8] {'pw'}, use_global_device_ids=true, to_apply=%region_1.1 | all-reduce | flops 64 | bytes 512 | tf_op jit(solution)/shard_map/while/body/eval_jaxpr/psum | solution.py:16
  1015.3 17.2 %psum.15 = f32[1,64]{1,0:T(1,128)S(1)} all-reduce(f32[1,64]{1,0:T(1,128)S(1)} %broadcast_select_fusion.2), channel_id=1, replica_groups=mesh['band'=16,'pw'=8] {'pw'}, use_global_device_ids=true, to_apply=%region_1.1 | all-reduce | flops 64 | bytes 512 | tf_op jit(solution)/shard_map/while/body/eval_jaxpr/psum | solution.py:16
  1053.8 17.2 %psum.15 = f32[1,64]{1,0:T(1,128)S(1)} all-reduce(f32[1,64]{1,0:T(1,128)S(1)} %broadcast_select_fusion.2), channel_id=1, replica_groups=mesh['band'=16,'pw'=8] {'pw'}, use_global_device_ids=true, to_apply=%region_1.1 | all-reduce | flops 64 | bytes 512 | tf_op jit(solution)/shard_map/while/body/eval_jaxpr/psum | solution.py:16
  1092.3 17.0 %psum.15 = f32[1,64]{1,0:T(1,128)S(1)} all-reduce(f32[1,64]{1,0:T(1,128)S(1)} %broadcast_select_fusion.2), channel_id=1, replica_groups=mesh['band'=16,'pw'=8] {'pw'}, use_global_device_ids=true, to_apply=%region_1.1 | all-reduce | flops 64 | bytes 512 | tf_op jit(solution)/shard_map/while/body/eval_jaxpr/psum | solution.py:16
  1130.6 17.0 %psum.15 = f32[1,64]{1,0:T(1,128)S(1)} all-reduce(f32[1,64]{1,0:T(1,128)S(1)} %broadcast_select_fusion.2), channel_id=1, replica_groups=mesh['band'=16,'pw'=8] {'pw'}, use_global_device_ids=true, to_apply=%region_1.1 | all-reduce | flops 64 | bytes 512 | tf_op jit(solution)/shard_map/while/body/eval_jaxpr/psum | solution.py:16
  1169.0 17.4 %psum.15 = f32[1,64]{1,0:T(1,128)S(1)} all-reduce(f32[1,64]{1,0:T(1,128)S(1)} %broadcast_select_fusion.2), channel_id=1, replica_groups=mesh['band'=16,'pw'=8] {'pw'}, use_global_device_ids=true, to_apply=%region_1.1 | all-reduce | flops 64 | bytes 512 | tf_op jit(solution)/shard_map/while/body/eval_jaxpr/psum | solution.py:16
  1206.6 59.4 %reshape.170 = f32[61440,1,2]{2,1,0:T(1,128)} reshape(f32[16,7680]{1,0:T(8,128)S(1)} %reduce.1) | data formatting | bytes 983040
  1266.0 16.7 %copy.90 = f32[1,2,16,3840]{3,2,1,0:T(8,128)S(1)} copy(f32[1,2,16,3840]{1,3,2,0:T(8,128)} %bitcast.125) | data formatting | bytes 983040 | tf_op jit(solution)/shard_map/all_to_all | solution.py:96
  1286.0 88.9 %all_to_all.66 = f32[64,2,3840]{2,1,0:T(2,128)S(1)} all-to-all(f32[64,2,3840]{2,1,0:T(2,128)S(1)} %copy.65), channel_id=1, replica_groups=mesh['band'=16,'pw'=8] {'band'}, dimensions={0} | all-to-all | bytes 3932160 | tf_op jit(solution)/shard_map/all_to_all | solution.py:98
  (95 shorter events, 161.0 us)
Async XLA Ops:
  225.9 8.5 copy-start.2
  225.9 27.2 %all-to-all-start = ((f32[1,2,12,96,96]{4,1,2,0,3:T(2,128)}), f32[1,2,12,96,96]{4,1,2,0,3:T(2,128)S(1)}, u32[]{:S(2)}, u32[]{:S(2)}) async-start(f32[1,2,12,96,96]{4,1,2,0,3:T(2,128)} %copy.52), calls=%async_computation | async-start | bytes 2359296 | tf_op jit(solution)/shard_map/all_to_all | solution.py:70
  258.3 4.2 copy-start
  258.3 22.9 %all-to-all-start.1 = ((f32[1,2,96,12,96]{4,1,3,0,2:T(2,128)}), f32[1,2,96,12,96]{4,1,3,0,2:T(2,128)S(1)}, u32[]{:S(2)}, u32[]{:S(2)}) async-start(f32[1,2,96,12,96]{4,1,3,0,2:T(2,128)} %copy.56), calls=%async_computation.1 | async-start | bytes 2359296 | tf_op jit(solution)/shard_map/all_to_all | solution.py:76
  531.7 16.5 %copy-start.1 = (bf16[1,2,61440]{2,1,0:T(2,128)(2,1)S(1)}, bf16[1,2,61440]{2,1,0:T(2,128)(2,1)}, u32[]{:S(2)}) copy-start(bf16[1,2,61440]{2,1,0:T(2,128)(2,1)} %param.7) | copy-start | bytes 737284
  865.8 31.3 %copy-start.3 = (f32[2,64]{1,0:T(2,128)S(1)}, f32[2,64]{1,0:T(2,128)}, u32[]{:S(2)}) copy-start(f32[2,64]{1,0:T(2,128)} %param.10) | copy-start | bytes 1540
  865.8 31.3 %copy-start.4 = (s32[16]{0:T(128)S(1)}, s32[16]{0:T(128)}, u32[]{:S(2)}) copy-start(s32[16]{0:T(128)} %param.11) | copy-start | bytes 196
  891.5 313.2 %all-to-all-start.2 = ((f32[16,1,7680]{2,1,0:T(1,128)}), f32[16,1,7680]{2,1,0:T(1,128)S(1)}, u32[]{:S(2)}, u32[]{:S(2)}) async-start(f32[16,1,7680]{2,1,0:T(1,128)} %reshape.169), calls=%async_computation.2 | async-start | bytes 983040 | tf_op jit(solution)/shard_map/all_to_all | solution.py:96
where the time goes:
time: 1390 us; the launch traced here: 1380 us
  local copies, waits for them, and re-layouts  644 us (46%)
  blocking collectives  350 us (25%)
  other arithmetic  279 us (20%)
  loops' own time  36.7 us (3%)
  waiting for transfers between devices  36.5 us (3%)
  starting transfers between devices  18.2 us (1%)
    unnamed x1, other arithmetic  273 us
    psum x16, blocking collectives, broadcast(): return lax.psum(block, axis)  261 us
    gather x2, local copies, waits for them, and re-layouts, shards(): back = planes.reshape(band_count, 2, slab_cells)[:, :, local_index]  236 us
    scatter x1, local copies, waits for them, and re-layouts, shards(): jnp.zeros((band_count, 2, slab_cells), jnp.float32).at[:, :, local_index]  172 us
    all_to_all x1, blocking collectives, shards(): lax.all_to_all(combined, 'band', split_axis=0, concat_axis=2, tiled=True)  88.9 us
    unnamed x14, local copies, waits for them, and re-layouts  85.9 us
    add x1, local copies, waits for them, and re-layouts, shards(): applied = kinetic_term[None, None] * values + back  43.8 us
    another operation x1, loops' own time, shards(): lax.fori_loop(0, panel_total, receive, jnp.zeros((panel_rows * panel_tota...  36.7 us
  transfers between devices with their start and end apart: 3, of which 2 were waited for; matrix products, arithmetic and copies ran while one was open for 1% of the time, Pallas kernels for 0%

commit v1 on v0

v1 whole, which is shorter than its diff:
```python
import math

import jax
import jax.numpy as jnp
import numpy as np
from jax import lax
from jax.experimental import pallas as pl
from jax.experimental.pallas import tpu as pltpu
from jax.sharding import PartitionSpec as P
import ml_dtypes

NG = 96
PARTS = 8
PLANES = NG // PARTS
GRID_ROWS = PLANES * NG
PIECE = PLANES * PLANES
PACKED = 480
CHIPS = 8
CHUNK = 2 * PACKED // CHIPS
BANDS = 16
OUT_LOCAL = 4
GUARD = 512
BLOCK = 48
FLAG = 1 << 20
MESH = pl.DeviceIdType.MESH
VMEM_SPEC = pl.BlockSpec(memory_space=pltpu.VMEM)
SMEM_SPEC = pl.BlockSpec(memory_space=pltpu.SMEM)
VMEM_BYTES = 48 * 1024 * 1024


def split_table(table):
    high = table.astype(ml_dtypes.bfloat16)
    low = (table - high.astype(np.float64)).astype(ml_dtypes.bfloat16)
    return np.stack([high, low])


def tables(direction):
    counter = np.arange(NG)
    angles = 2.0 * math.pi / NG * (np.outer(counter, counter) % NG)
    cosines = np.cos(angles) / math.sqrt(NG)
    sines = direction * np.sin(angles) / math.sqrt(NG)
    right = np.zeros((256, 256))
    right[:NG, :NG] = cosines
    right[128 : 128 + NG, :NG] = -sines
    right[:NG, 128 : 128 + NG] = sines
    right[128 : 128 + NG, 128 : 128 + NG] = cosines
    left = np.concatenate([cosines, sines], axis=0)
    padded = np.zeros((2, PARTS, 16, NG))
    padded[:, :, :PLANES] = left.reshape(2, PARTS, PLANES, NG)
    return split_table(right), split_table(left), split_table(padded.reshape(256, NG))


def split(value):
    high = value.astype(jnp.bfloat16)
    return high, (value - high.astype(jnp.float32)).astype(jnp.bfloat16)


def dot(a, b):
    return jnp.dot(a, b, preferred_element_type=jnp.float32)


def left_transform(table_ref, field):
    high, low = split(field)
    product = dot(table_ref[0], high) + dot(table_ref[0], low) + dot(table_ref[1], high)
    half = product.shape[0] // 2
    real = product[:half, :128] - product[half:, 128:]
    imag = product[:half, 128:] + product[half:, :128]
    return real, imag


def right_transform(table_ref, field):
    high, low = split(field)
    return dot(high, table_ref[0]) + dot(low, table_ref[0]) + dot(high, table_ref[1])


def cell_of(index):
    line = ((index.astype(jnp.float32) + 0.5) * (1.0 / NG)).astype(jnp.int32)
    return line, index - NG * line


def spread_kernel(index_ref, wave_ref, right_ref, padded_ref, real_ref, imag_ref, gap_ref, vr, vi, gap):
    first_line = lax.axis_index("pw") * GRID_ROWS
    lane = lax.broadcasted_iota(jnp.int32, (BLOCK, 128), 1)
    rows = lax.broadcasted_iota(jnp.int32, (BLOCK, 128), 0)
    zero = jnp.zeros((BLOCK, 128), jnp.float32)
    total = GUARD + GRID_ROWS

    def clear(step, carry):
        at = pl.ds(pl.multiple_of(step * 64, 64), 64)
        vr[at, :] = jnp.zeros((64, 128), jnp.float32)
        vi[at, :] = jnp.zeros((64, 128), jnp.float32)
        gap[at, :] = jnp.zeros((64, 128), jnp.int32)
        return carry

    lax.fori_loop(0, total // 64, clear, 0)

    def place(step, carry):
        base = pl.multiple_of(step * BLOCK, BLOCK)
        line, z = cell_of(index_ref[pl.ds(base, BLOCK), :])
        position = (rows + base) * 128 + lane
        at = pl.ds(pl.multiple_of(GUARD + base, 16), BLOCK)
        gap[at, :] = ((line - first_line) * 128 + z - position) | FLAG
        vr[at, :] = wave_ref[pl.ds(2 * base, BLOCK, stride=2), :]
        vi[at, :] = wave_ref[pl.ds(2 * base + 1, BLOCK, stride=2), :]
        return carry

    lax.fori_loop(0, PACKED // BLOCK, place, 0)

    steps = GRID_ROWS // BLOCK
    for bit in range(16, -1, -1):
        shift = 1 << bit

        def move(step, carry, shift=shift):
            base = GUARD + (steps - 1 - step) * BLOCK
            here = pl.ds(pl.multiple_of(base, 16), BLOCK)
            if shift >= 128:
                there = pl.ds(base - shift // 128, BLOCK)
            else:
                there = pl.ds(base - 1, BLOCK)
            own = [ref[here, :] for ref in (gap, vr, vi)]
            other = [ref[there, :] for ref in (gap, vr, vi)]
            if shift < 128:
                stay = lane < 128 - shift
                other = [pltpu.roll(jnp.where(stay, a, b), shift, 1) for a, b in zip(own, other)]
            arrives = (other[0] & shift) != 0
            left = jnp.where((own[0] & shift) != 0, 0, own[0])
            gap[here, :] = jnp.where(arrives, other[0], left)
            vr[here, :] = jnp.where(arrives, other[1], own[1])
            vi[here, :] = jnp.where(arrives, other[2], own[2])
            return carry

        lax.fori_loop(0, steps, move, 0)

    for x in range(PLANES):
        at = pl.ds(GUARD + x * NG, NG)
        held = gap[at, :]
        gap_ref[pl.ds(x * NG, NG), :] = held
        filled = (held & FLAG) != 0
        field = jnp.concatenate(
            [jnp.where(filled, vr[at, :], 0.0), jnp.where(filled, vi[at, :], 0.0)], axis=1
        ).astype(jnp.bfloat16)
        field = dot(field, right_ref[0]) + dot(field, right_ref[1])
        real, imag = left_transform(padded_ref, field)
        for d in range(PARTS):
            at = pl.ds(d * PIECE + x * PLANES, PLANES)
            real_ref[at, :] = real[16 * d : 16 * d + PLANES]
            imag_ref[at, :] = imag[16 * d : 16 * d + PLANES]


def lines_kernel(
    send_real, send_imag, potential_ref, rotation_ref, inverse_ref, forward_ref,
    out_real, out_imag, rotations,
    got_real, got_imag, back_real, back_imag, send_sem, recv_sem, own_sem,
):
    me = lax.axis_index("pw")
    barrier = pltpu.get_barrier_semaphore()
    for turn in range(1, PARTS):
        pl.semaphore_signal(
            barrier, inc=1, device_id={"pw": lax.rem(me + turn, PARTS)}, device_id_type=MESH
        )
    pl.semaphore_wait(barrier, PARTS - 1)

    def piece(ref, which):
        return ref.at[pl.ds(pl.multiple_of(which * PIECE, PIECE), PIECE), :]

    def exchange(phase, sources, targets):
        copies = []
        for turn in range(1, PARTS):
            peer = lax.rem(me + turn, PARTS)
            for part, (source, target) in enumerate(zip(sources, targets)):
                copy = pltpu.make_async_remote_copy(
                    src_ref=piece(source, peer),
                    dst_ref=piece(target, me),
                    send_sem=send_sem.at[phase, part, turn],
                    recv_sem=recv_sem.at[phase, part, turn],
                    device_id={"pw": peer},
                    device_id_type=MESH,
                )
                copy.start()
                copies.append(copy)
        for part, (source, target) in enumerate(zip(sources, targets)):
            copy = pltpu.make_async_copy(piece(source, me), piece(target, me), own_sem.at[phase, part])
            copy.start()
            copies.append(copy)
        return copies

    small = []
    for turn in range(1, PARTS):
        copy = pltpu.make_async_remote_copy(
            src_ref=rotation_ref,
            dst_ref=rotations.at[me],
            send_sem=send_sem.at[2, 0, turn],
            recv_sem=recv_sem.at[2, 0, turn],
            device_id={"pw": lax.rem(me + turn, PARTS)},
            device_id_type=MESH,
        )
        copy.start()
        small.append(copy)
    copy = pltpu.make_async_copy(rotation_ref, rotations.at[me], own_sem.at[2, 0])
    copy.start()
    small.append(copy)

    first = exchange(0, (send_real, send_imag), (got_real, got_imag))
    for copy in first:
        copy.wait()
    for b in range(PLANES):
        column = pl.ds(b, NG, stride=PLANES)
        field = jnp.concatenate([got_real[column, :], got_imag[column, :]], axis=1)
        real, imag = left_transform(inverse_ref, field)
        offset = b * NG % 128
        start = b * NG - offset
        if offset + NG > 128:
            local = pltpu.roll(potential_ref[:, start : start + 256], 256 - offset, 1)[:, :128]
        else:
            local = potential_ref[:, start : start + 128]
            if offset:
                local = pltpu.roll(local, 128 - offset, 1)
        field = jnp.concatenate([local * real, local * imag], axis=1)
        real, imag = left_transform(forward_ref, field)
        back_real[column, :] = real
        back_imag[column, :] = imag
    second = exchange(1, (back_real, back_imag), (out_real, out_imag))
    for copy in second + small:
        copy.wait()


def pick_kernel(
    back_real, back_imag, gap_ref, wave_ref, index_ref, left_ref, right_ref, applied_ref,
    plane_real, plane_imag, vr, vi, gap,
):
    lane = lax.broadcasted_iota(jnp.int32, (BLOCK, 128), 1)
    for x in range(PLANES):
        for d in range(PARTS):
            source = pl.ds(d * PIECE + x * PLANES, PLANES)
            target = pl.ds(d * PLANES, PLANES)
            plane_real[x, target, :] = back_real[source, :]
            plane_imag[x, target, :] = back_imag[source, :]
        field = jnp.concatenate([plane_real[x], plane_imag[x]], axis=1)
        real, imag = left_transform(left_ref, field)
        field = right_transform(right_ref, jnp.concatenate([real, imag], axis=1))
        at = pl.ds(x * NG, NG)
        vr[at, :] = field[:, :128]
        vi[at, :] = field[:, 128:]
        gap[at, :] = gap_ref[at, :]

    def clear(step, carry):
        at = pl.ds(pl.multiple_of(GRID_ROWS + step * 64, 64), 64)
        gap[at, :] = jnp.zeros((64, 128), jnp.int32)
        vr[at, :] = jnp.zeros((64, 128), jnp.float32)
        vi[at, :] = jnp.zeros((64, 128), jnp.float32)
        return carry

    lax.fori_loop(0, GUARD // 64, clear, 0)
    steps = GRID_ROWS // BLOCK
    for bit in range(17):
        shift = 1 << bit

        def move(step, carry, shift=shift):
            base = step * BLOCK
            here = pl.ds(pl.multiple_of(base, 16), BLOCK)
            if shift >= 128:
                there = pl.ds(base + shift // 128, BLOCK)
            else:
                there = pl.ds(base + 1, BLOCK)
            own = [ref[here, :] for ref in (gap, vr, vi)]
            other = [ref[there, :] for ref in (gap, vr, vi)]
            if shift < 128:
                stay = lane >= shift
                other = [pltpu.roll(jnp.where(stay, a, b), 128 - shift, 1) for a, b in zip(own, other)]
            arrives = (other[0] & shift) != 0
            left = jnp.where((own[0] & shift) != 0, 0, own[0])
            gap[here, :] = jnp.where(arrives, other[0], left)
            vr[here, :] = jnp.where(arrives, other[1], own[1])
            vi[here, :] = jnp.where(arrives, other[2], own[2])
            return carry

        lax.fori_loop(0, steps, move, 0)

    def signed_square(position):
        signed = jnp.where(position < NG // 2, position, position - NG).astype(jnp.float32)
        return signed * signed

    def finish(step, carry):
        base = pl.multiple_of(step * BLOCK, BLOCK)
        line, z = cell_of(index_ref[pl.ds(base, BLOCK), :])
        x, y = cell_of(line)
        energy = 2.0 * (signed_square(x) + signed_square(y) + signed_square(z)) / float((NG // 2) ** 2)
        for part, ref in enumerate((vr, vi)):
            at = pl.ds(2 * base + part, BLOCK, stride=2)
            applied_ref[at, :] = energy * wave_ref[at, :] + ref[pl.ds(base, BLOCK), :]
        return carry

    lax.fori_loop(0, PACKED // BLOCK, finish, 0)


def rotate_kernel(
    applied_ref, rotations, order_ref, out_ref,
    window, mixed, send_sem, recv_sem, pair_send, pair_recv, own_sem,
):
    band = lax.axis_index("band")
    chip, core = band // 2, band % 2
    sibling = {"band": chip * 2 + 1 - core}
    barrier = pltpu.get_barrier_semaphore()
    pl.semaphore_signal(barrier, inc=1, device_id=sibling, device_id_type=MESH)
    for turn in range(1, CHIPS):
        peer = lax.rem(chip + turn, CHIPS)
        pl.semaphore_signal(barrier, inc=1, device_id={"band": peer * 2 + core}, device_id_type=MESH)
    pl.semaphore_wait(barrier, CHIPS)

    def rows(which):
        return pl.ds(pl.multiple_of(which * CHUNK, CHUNK), CHUNK)

    own = pltpu.make_async_copy(applied_ref.at[rows(chip), :], window.at[band], own_sem.at[0])
    own.start()
    sent = []
    for turn in range(1, CHIPS):
        peer = lax.rem(chip + turn, CHIPS)
        copy = pltpu.make_async_remote_copy(
            src_ref=applied_ref.at[rows(peer), :],
            dst_ref=window.at[band],
            send_sem=send_sem.at[0, turn],
            recv_sem=recv_sem.at[0, turn],
            device_id={"band": peer * 2 + core},
            device_id_type=MESH,
        )
        copy.start()
        sent.append(copy)

    pairs = []

    def pass_on(source, turn):
        copy = pltpu.make_async_remote_copy(
            src_ref=window.at[source],
            dst_ref=window.at[source],
            send_sem=pair_send.at[turn],
            recv_sem=pair_recv.at[turn],
            device_id=sibling,
            device_id_type=MESH,
        )
        copy.start()
        pairs.append(copy)

    own.wait()
    pass_on(band, 0)
    for turn in range(1, CHIPS):
        sent[turn - 1].wait_recv()
        pass_on(lax.rem(chip - turn + CHIPS, CHIPS) * 2 + core, turn)
    for copy in pairs:
        copy.wait()
    for copy in sent:
        copy.wait_send()

    results = []
    for turn in range(1, CHIPS + 1):
        peer = lax.rem(chip + turn, CHIPS)

        def mix(step, carry, turn=turn, peer=peer):
            at = pl.ds(pl.multiple_of(step * 24, 24), 24)
            totals = [None] * OUT_LOCAL
            for i in range(BANDS):
                panel = order_ref[i]
                term = window[i, at, :]
                for j in range(OUT_LOCAL):
                    factor = rotations[panel // 2, panel % 2, (peer * 2 + core) * OUT_LOCAL + j]
                    totals[j] = factor * term if i == 0 else totals[j] + factor * term
            for j in range(OUT_LOCAL):
                mixed[turn - 1, j, at, :] = totals[j]
            return carry

        lax.fori_loop(0, CHUNK // 24, mix, 0)
        target = out_ref.at[:, rows(chip), :]
        if turn < CHIPS:
            copy = pltpu.make_async_remote_copy(
                src_ref=mixed.at[turn - 1],
                dst_ref=target,
                send_sem=send_sem.at[1, turn],
                recv_sem=recv_sem.at[1, turn],
                device_id={"band": peer * 2 + core},
                device_id_type=MESH,
            )
        else:
            copy = pltpu.make_async_copy(mixed.at[turn - 1], target, own_sem.at[1])
        copy.start()
        results.append(copy)
    for copy in results:
        copy.wait()


def shards(wave_coeffs, potential, sphere_index, rotation, panel_order):
    f32 = jnp.float32
    values = wave_coeffs.astype(f32).reshape(2, PACKED, 128).transpose(1, 0, 2).reshape(2 * PACKED, 128)
    index = sphere_index.reshape(PACKED, 128)
    inverse_right, inverse_left, inverse_padded = tables(1.0)
    forward_right, forward_left, _ = tables(-1.0)
    grid_shape = jax.ShapeDtypeStruct((GRID_ROWS, 128), f32)
    grid_buffer = pltpu.VMEM((GRID_ROWS, 128), f32)
    dma = pltpu.SemaphoreType.DMA

    def wide(kind):
        return pltpu.VMEM((GUARD + GRID_ROWS, 128), kind)

    real, imag, gap = pl.pallas_call(
        spread_kernel,
        out_shape=(grid_shape, grid_shape, jax.ShapeDtypeStruct((GRID_ROWS, 128), jnp.int32)),
        in_specs=[VMEM_SPEC] * 4,
        out_specs=[VMEM_SPEC] * 3,
        scratch_shapes=[wide(f32), wide(f32), wide(jnp.int32)],
        compiler_params=pltpu.CompilerParams(vmem_limit_bytes=VMEM_BYTES),
        name="spread",
    )(index, values, jnp.asarray(inverse_right), jnp.asarray(inverse_padded))
    real, imag, rotations = pl.pallas_call(
        lines_kernel,
        out_shape=(grid_shape, grid_shape, jax.ShapeDtypeStruct((PARTS, 2, 64), f32)),
        in_specs=[VMEM_SPEC] * 6,
        out_specs=[VMEM_SPEC] * 3,
        scratch_shapes=[grid_buffer] * 4
        + [dma((3, 2, PARTS)), dma((3, 2, PARTS)), dma((3, 2))],
        compiler_params=pltpu.CompilerParams(
            vmem_limit_bytes=VMEM_BYTES, collective_id=0, has_side_effects=True
        ),
        name="lines",
    )(real, imag, potential, rotation, jnp.asarray(inverse_left), jnp.asarray(forward_left))
    plane = pltpu.VMEM((PLANES, NG, 128), f32)
    applied = pl.pallas_call(
        pick_kernel,
        out_shape=jax.ShapeDtypeStruct((2 * PACKED, 128), f32),
        in_specs=[VMEM_SPEC] * 7,
        out_specs=VMEM_SPEC,
        scratch_shapes=[plane, plane, wide(f32), wide(f32), wide(jnp.int32)],
        compiler_params=pltpu.CompilerParams(vmem_limit_bytes=VMEM_BYTES),
        name="pick",
    )(real, imag, gap, values, index, jnp.asarray(forward_left), jnp.asarray(forward_right))
    out = pl.pallas_call(
        rotate_kernel,
        out_shape=jax.ShapeDtypeStruct((OUT_LOCAL, 2 * PACKED, 128), f32),
        in_specs=[VMEM_SPEC, SMEM_SPEC, SMEM_SPEC],
        out_specs=VMEM_SPEC,
        scratch_shapes=[
            pltpu.VMEM((BANDS, CHUNK, 128), f32),
            pltpu.VMEM((CHIPS, OUT_LOCAL, CHUNK, 128), f32),
            dma((2, CHIPS)),
            dma((2, CHIPS)),
            dma((CHIPS,)),
            dma((CHIPS,)),
            dma((2,)),
        ],
        compiler_params=pltpu.CompilerParams(
            vmem_limit_bytes=VMEM_BYTES, collective_id=1, has_side_effects=True
        ),
        name="rotate",
    )(applied, rotations, panel_order)
    return out.reshape(OUT_LOCAL, PACKED, 2, 128).transpose(0, 2, 1, 3).reshape(OUT_LOCAL, 2, PACKED * 128)


def solution(mesh):
    return jax.shard_map(
        shards,
        mesh=mesh,
        in_specs=(P("band", None, "pw"), P(None, "pw"), P("pw"), P("pw", None), P()),
        out_specs=P("band", None, "pw"),
        check_vma=False,
    )
```

time: 1390 us -> 140 us (0.10)
  local copies, waits for them, and re-layouts: 644 us -> 6.54 us
  blocking collectives: 350 us -> 0 us
  other arithmetic: 279 us -> 1.18 us
  Pallas kernels: 0 us -> 132 us
  loops' own time: 36.7 us -> 0 us
  waiting for transfers between devices: 36.5 us -> 0 us
  starting transfers between devices: 18.2 us -> 0 us
    unnamed x1 -> x0, other arithmetic: 273 us -> none
    psum x16 -> x0, blocking collectives: 261 us -> none  [broadcast(): return lax.psum(block, axis)]
    gather x2 -> x0, local copies, waits for them, and re-layouts: 236 us -> none  [shards(): back = planes.reshape(band_count, 2, slab_cells)[:, :, local_index]]
    scatter x1 -> x0, local copies, waits for them, and re-layouts: 172 us -> none  [shards(): jnp.zeros((band_count, 2, slab_cells), jnp.float32).at[:, :, local_index]]
    pallas_call x0 -> x4, Pallas kernels: none -> 132 us  [the longest x1 46.2 us: shards(): pl.pallas_call(rotate_kernel, out_shape=jax.ShapeDtypeStruct((OUT_LOCAL,...]
    all_to_all x1 -> x0, blocking collectives: 88.9 us -> none  [shards(): lax.all_to_all(combined, 'band', split_axis=0, concat_axis=2, tiled=True)]
    unnamed x14 -> x21, local copies, waits for them, and re-layouts: 85.9 us -> 6.54 us
    add x1 -> x0, local copies, waits for them, and re-layouts: 43.8 us -> none  [shards(): applied = kinetic_term[None, None] * values + back]
  transfers between devices with their start and end apart: 3 -> 0, of which waited for: 2 -> 0; matrix products, arithmetic and copies ran while one was open for 1% -> 0% of each run, Pallas kernels for 0% -> 0%
where the time goes in v1:
time: 140 us
  Pallas kernels  132 us (94%)
  local copies, waits for them, and re-layouts  6.54 us (5%)
    pallas_call x1, Pallas kernels, shards(): pl.pallas_call(rotate_kernel, out_shape=jax.ShapeDtypeStruct((OUT_LOCAL,...  46.2 us
    pallas_call x1, Pallas kernels, shards(): pl.pallas_call(lines_kernel, out_shape=(grid_shape, grid_shape, jax.Shape...  42.7 us
    pallas_call x1, Pallas kernels, shards(): pl.pallas_call(pick_kernel, out_shape=jax.ShapeDtypeStruct((2 * PACKED, 1...  22.2 us
    pallas_call x1, Pallas kernels, shards(): pl.pallas_call(spread_kernel, out_shape=(grid_shape, grid_shape, jax.Shap...  20.8 us
    unnamed x21, local copies, waits for them, and re-layouts  6.54 us

profile of v1, /device:TPU:1, one launch (start us, length us, event | category | flops | bytes accessed | tf_op | source)
XLA Modules:
  0.0 139.8 jit_solution(1275941032371629019)
XLA Ops:
  0.0 0.0 copy-start.1
  0.0 0.0 copy-start.2
  0.0 1.2 bitcast_convert_fusion
  1.2 0.0 copy-start
  1.2 0.9 copy-done
  2.1 0.0 copy-start.5
  2.1 0.9 copy-done.5
  3.1 0.0 copy-start.6
  3.1 0.9 copy-done.6
  4.0 0.0 copy-start.4
  4.0 20.8 %spread.1 = (f32[1152,128]{1,0:T(8,128)S(1)}, f32[1152,128]{1,0:T(8,128)S(1)}, s32[1152,128]{1,0:T(8,128)S(1)}) custom-call(s32[480,128]{1,0:T(8,128)S(1)} %bitcast.15, f32[960,128]{1,0:T(8,128)S(1)} %bitcast.13, bf16[2,256,256]{2,1,0:T(8,128)(2,1)S(1)} %copy-done.5, bf16[2,256,96]{2,1,0:T(8,128)(2,1)S(1)} %copy-done.6), custom_call_target="tpu_custom_call" | custom-call | tf_op jit(solution)/shard_map/spread/pallas_call | solution.py:402
  24.8 0.0 copy-done.2
  24.8 0.0 copy-start.3
  24.8 0.9 copy-done.3
  25.7 0.9 copy-done.7
  26.6 0.7 copy-done.8
  27.3 42.7 %lines.1 = (f32[1152,128]{1,0:T(8,128)S(1)}, f32[1152,128]{1,0:T(8,128)S(1)}, f32[8,2,64]{2,1,0:T(2,128)S(1)}) custom-call(f32[1152,128]{1,0:T(8,128)S(1)} %get-tuple-element.11.send_real, f32[1152,128]{1,0:T(8,128)S(1)} %get-tuple-element.12.send_imag, f32[96,1152]{1,0:T(8,128)S(1)} %copy-done.2, f32[2,64]{1,0:T(2,128)S(1)} %copy-done.8, ...), custom_call_target="tpu_custom_call" | custom-call | tf_op jit(solution)/shard_map/lines/pallas_call | solution.py:411
  70.0 0.0 copy-start.9
  70.1 0.0 copy-done.1
  70.1 0.0 copy-done.4
  70.1 22.2 %pick.1.applied_ref = f32[960,128]{1,0:T(8,128)S(1)} custom-call(f32[1152,128]{1,0:T(8,128)S(1)} %get-tuple-element.13.back_real, f32[1152,128]{1,0:T(8,128)S(1)} %get-tuple-element.14.back_imag, s32[1152,128]{1,0:T(8,128)S(1)} %get-tuple-element.15.gap_ref, f32[960,128]{1,0:T(8,128)S(1)} %bitcast.14, s32[480,128]{1,0:T(8,128)S(1)} %bitcast.16, ...), custom_call_target="tpu_custom_call" | custom-call | tf_op jit(solution)/shard_map/pick/pallas_call | solution.py:424
  92.3 0.0 copy-done.9
  92.3 46.2 %rotate.1 = f32[4,960,128]{2,1,0:T(8,128)S(1)} custom-call(f32[960,128]{1,0:T(8,128)S(1)} %pick.1.applied_ref, f32[8,2,64]{2,1,0:T(2,128)S(1)} %get-tuple-element.16.rotations, s32[16]{0:T(128)S(1)} %copy-done.9), custom_call_target="tpu_custom_call" | custom-call | tf_op jit(solution)/shard_map/rotate/pallas_call | solution.py:433
  138.5 1.3 copy.14
  (2 shorter events, 0.0 us)
Async XLA Ops:
  0.0 70.1 %copy-start.1 = (s32[61440]{0:T(1024)S(1)}, s32[61440]{0:T(1024)}, u32[]{:S(2)}) copy-start(s32[61440]{0:T(1024)} %param.12) | copy-start | bytes 737284
  0.0 24.8 %copy-start.2 = (f32[96,1152]{1,0:T(8,128)S(1)}, f32[96,1152]{1,0:T(8,128)}, u32[]{:S(2)}) copy-start(f32[96,1152]{1,0:T(8,128)} %potential_ref.1) | copy-start | bytes 1327108
  1.2 0.9 copy-start
  2.1 0.9 copy-start.5
  3.1 0.9 copy-start.6
  4.0 66.1 %copy-start.4 = (bf16[2,256,256]{2,1,0:T(8,128)(2,1)S(1)}, bf16[2,256,256]{2,1,0:T(8,128)(2,1)}, u32[]{:S(2)}) copy-start(bf16[2,256,256]{2,1,0:T(8,128)(2,1)} %constant.14.clone.right_ref) | copy-start | bytes 786436
  24.8 0.9 copy-start.3
  25.7 0.9 copy-start.7
  26.6 0.7 copy-start.8
  70.0 22.2 %copy-start.9 = (s32[16]{0:T(128)S(1)}, s32[16]{0:T(128)}, u32[]{:S(2)}) copy-start(s32[16]{0:T(128)} %order_ref.1) | copy-start | bytes 196

commit v2 on v0

v2 whole, which is shorter than its diff:
```python
import math

import jax
import jax.numpy as jnp
import numpy as np
from jax import lax
from jax.experimental import pallas as pl
from jax.experimental.pallas import tpu as pltpu
from jax.sharding import PartitionSpec as P
import ml_dtypes

NG = 96
PARTS = 8
PLANES = NG // PARTS
GRID_ROWS = PLANES * NG
GROUPS = 3
SENT = 72
GROUP_ROWS = PARTS * SENT
PACKED = 480
CHIPS = 8
CHUNK = 2 * PACKED // CHIPS
PIECES = 3
PIECE = CHUNK // PIECES
BANDS = 16
OUT_LOCAL = 4
GUARD = 512
BLOCK = 96
FLAG = 1 << 20
MESH = pl.DeviceIdType.MESH
VMEM_SPEC = pl.BlockSpec(memory_space=pltpu.VMEM)
SMEM_SPEC = pl.BlockSpec(memory_space=pltpu.SMEM)
HBM_SPEC = pl.BlockSpec(memory_space=pltpu.HBM)
VMEM_BYTES = 48 * 1024 * 1024


def split_table(table):
    high = table.astype(ml_dtypes.bfloat16)
    low = (table - high.astype(np.float64)).astype(ml_dtypes.bfloat16)
    return np.stack([high, low])


def stacked_table(direction, rows, columns):
    row_part, row_at = np.array(rows).T
    column_part, column_at = np.array(columns).T
    angles = 2.0 * math.pi / NG * (np.outer(row_at, column_at) % NG)
    cosines = np.cos(angles) / math.sqrt(NG)
    sines = direction * np.sin(angles) / math.sqrt(NG)
    same = row_part[:, None] == column_part[None, :]
    signs = np.where(row_part == 0, -1.0, 1.0)[:, None]
    return np.where(same, cosines, signs * sines)


def orders():
    natural = [(p, n) for p in range(2) for n in range(NG)]
    sent_y = [(p, PLANES * d + b) for p in range(2) for b in range(PLANES) for d in range(PARTS)]
    got_x = [
        (p, PLANES * s + 4 * g + t)
        for t in range(4) for g in range(GROUPS) for s in range(PARTS) for p in range(2)
    ]
    back_x = [
        (p, PLANES * e + 4 * g + t)
        for t in range(4) for e in range(PARTS) for g in range(GROUPS) for p in range(2)
    ]
    fin_y = [
        (p, PLANES * s + 4 * h + b)
        for p in range(2) for b in range(4) for h in range(GROUPS) for s in range(PARTS)
    ]
    return natural, sent_y, got_x, back_x, fin_y


def left_tables():
    natural, sent_y, got_x, back_x, fin_y = orders()
    return np.stack([
        split_table(stacked_table(1.0, sent_y, natural)),
        split_table(stacked_table(1.0, natural, got_x)),
        split_table(stacked_table(-1.0, back_x, natural)),
        split_table(stacked_table(-1.0, natural, fin_y)),
    ])


def right_tables():
    natural = orders()[0]
    stack = []
    for direction in (1.0, -1.0):
        table = stacked_table(direction, natural, natural).T
        wide = np.zeros((256, 256))
        for p in range(2):
            for q in range(2):
                wide[128 * p : 128 * p + NG, 128 * q : 128 * q + NG] = table[
                    NG * p : NG * p + NG, NG * q : NG * q + NG
                ]
        stack.append(split_table(wide))
    return np.stack(stack)


def split(value):
    high = value.astype(jnp.bfloat16)
    return high, (value - high.astype(jnp.float32)).astype(jnp.bfloat16)


def dot(a, b):
    return jnp.dot(a, b, preferred_element_type=jnp.float32)


def left_transform(table_ref, which, field):
    high, low = split(field)
    return (
        dot(table_ref[which, 0], high) + dot(table_ref[which, 0], low) + dot(table_ref[which, 1], high)
    )


def right_transform(table_ref, which, field):
    high, low = split(field)
    return (
        dot(high, table_ref[which, 0]) + dot(low, table_ref[which, 0]) + dot(high, table_ref[which, 1])
    )


def cell_of(index):
    line = ((index.astype(jnp.float32) + 0.5) * (1.0 / NG)).astype(jnp.int32)
    return line, index - NG * line


def pack_fourth(lane, base, fourth, t):
    return jnp.where(lane < NG, base, pltpu.roll(fourth, NG - 32 * t, 1))


def unpack_fourth(lane, first, second, third):
    return jnp.where(
        lane < 32,
        pltpu.roll(first, 32, 1),
        jnp.where(lane < 64, pltpu.roll(second, 64, 1), pltpu.roll(third, 96, 1)),
    )


def spread_kernel(index_ref, wave_ref, real_ref, imag_ref, leave_ref, vr, vi, gap):
    first_line = lax.axis_index("pw") * GRID_ROWS
    lane = lax.broadcasted_iota(jnp.int32, (BLOCK, 128), 1)
    rows = lax.broadcasted_iota(jnp.int32, (BLOCK, 128), 0)
    gap[...] = jnp.zeros_like(gap)
    for ref in (vr, vi):
        ref[pl.ds(0, GUARD), :] = jnp.zeros((GUARD, 128), jnp.float32)
        ref[pl.ds(GUARD + PACKED, GRID_ROWS - PACKED), :] = jnp.zeros((GRID_ROWS - PACKED, 128), jnp.float32)
    for step in range(PACKED // BLOCK):
        base = step * BLOCK
        line, z = cell_of(index_ref[pl.ds(base, BLOCK), :])
        position = (rows + base) * 128 + lane
        at = pl.ds(GUARD + base, BLOCK)
        gap[at, :] = ((line - first_line) * 128 + z - position) | FLAG
        vr[at, :] = wave_ref[pl.ds(2 * base, BLOCK, stride=2), :]
        vi[at, :] = wave_ref[pl.ds(2 * base + 1, BLOCK, stride=2), :]

    for bit in range(16, -1, -1):
        shift = 1 << bit
        reach = min(PACKED + sum(1 << k for k in range(bit, 17)) // 128 + 1, GRID_ROWS)
        for step in reversed(range(GRID_ROWS // BLOCK)):
            base = step * BLOCK
            leave_at = pl.ds(base, BLOCK)
            if base >= reach:
                if bit == 16:
                    leave_ref[leave_at, :] = jnp.zeros((BLOCK, 128), jnp.int32)
                continue
            here = pl.ds(GUARD + base, BLOCK)
            there = pl.ds(GUARD + base - max(shift // 128, 1), BLOCK)
            own = [ref[here, :] for ref in (gap, vr, vi)]
            other = [ref[there, :] for ref in (gap, vr, vi)]
            if shift < 128:
                stay = lane < 128 - shift
                other = [pltpu.roll(jnp.where(stay, a, b), shift, 1) for a, b in zip(own, other)]
            arrives = (other[0] & shift) != 0
            leaves = own[0] & shift
            left = jnp.where(leaves != 0, 0, own[0])
            held = jnp.where(arrives, other[0], left)
            if bit == 16:
                leave_ref[leave_at, :] = leaves
            else:
                leave_ref[leave_at, :] = leave_ref[leave_at, :] | leaves
            values = [jnp.where(arrives, other[k], own[k]) for k in (1, 2)]
            if bit == 0:
                filled = (held & FLAG) != 0
                real_ref[leave_at, :] = jnp.where(filled, values[0], 0.0)
                imag_ref[leave_at, :] = jnp.where(filled, values[1], 0.0)
            else:
                gap[here, :] = held
                vr[here, :] = values[0]
                vi[here, :] = values[1]


def fields_kernel(
    real_ref, imag_ref, potential_hbm, rotation_ref, left_hbm, right_hbm,
    out_real, out_imag, rotations,
    potential_ref, left_ref, right_ref, send, got, back, fin,
    send_sem, recv_sem, own_sem, small_send, small_recv, load_sem,
):
    me = lax.axis_index("pw")
    peers = [lax.rem(me + turn, PARTS) for turn in range(PARTS)]
    loads = [
        pltpu.make_async_copy(source, target, load_sem.at[k])
        for k, (source, target) in enumerate(
            ((right_hbm, right_ref), (left_hbm, left_ref), (potential_hbm, potential_ref))
        )
    ]
    for load in loads:
        load.start()
    barrier = pltpu.get_barrier_semaphore()
    for peer in peers[1:]:
        pl.semaphore_signal(barrier, inc=1, device_id={"pw": peer}, device_id_type=MESH)

    def start_group(phase, group, source, target):
        copies = []
        for turn, peer in enumerate(peers):
            from_rows = pl.ds(pl.multiple_of(group * GROUP_ROWS + peer * SENT, SENT), SENT)
            to_rows = pl.ds(pl.multiple_of(group * GROUP_ROWS + me * SENT, SENT), SENT)
            if turn:
                copy = pltpu.make_async_remote_copy(
                    src_ref=source.at[from_rows, :],
                    dst_ref=target.at[to_rows, :],
                    send_sem=send_sem.at[phase, group, turn],
                    recv_sem=recv_sem.at[phase, group, turn],
                    device_id={"pw": peer},
                    device_id_type=MESH,
                )
            else:
                copy = pltpu.make_async_copy(
                    source.at[from_rows, :], target.at[to_rows, :], own_sem.at[phase, group]
                )
            copy.start()
            copies.append(copy)
        return copies

    loads[0].wait()
    loads[1].wait()
    lane = lax.broadcasted_iota(jnp.int32, (2 * NG, 128), 1)
    first = []
    for g in range(GROUPS):
        planes = []
        for pair in range(2):
            stacked = []
            for t in (2 * pair, 2 * pair + 1):
                at = pl.ds((4 * g + t) * NG, NG)
                field = jnp.concatenate([real_ref[at, :], imag_ref[at, :]], axis=1).astype(jnp.bfloat16)
                field = dot(field, right_ref[0, 0]) + dot(field, right_ref[0, 1])
                stacked.append(jnp.concatenate([field[:, :128], field[:, 128:]], axis=0))
            both = left_transform(left_ref, 0, jnp.concatenate(stacked, axis=1))
            planes += [both[:, :128], both[:, 128:]]
        for t in range(3):
            packed = pack_fourth(lane, planes[t], planes[3], t)
            for p in range(2):
                for b in range(PLANES):
                    row = (p * PLANES + b) * PARTS
                    at = pl.ds(g * GROUP_ROWS + (p * 3 + t) * PLANES + b, PARTS, stride=SENT)
                    send[at, :] = packed[row : row + PARTS]
        if g == 0:
            pl.semaphore_wait(barrier, PARTS - 1)
        first += start_group(0, g, send, got)

    small = []
    for turn, peer in enumerate(peers):
        if turn:
            copy = pltpu.make_async_remote_copy(
                src_ref=rotation_ref,
                dst_ref=rotations.at[me],
                send_sem=small_send.at[turn],
                recv_sem=small_recv.at[turn],
                device_id={"pw": peer},
                device_id_type=MESH,
            )
        else:
            copy = pltpu.make_async_copy(rotation_ref, rotations.at[me], load_sem.at[3])
        copy.start()
        small.append(copy)

    loads[2].wait()
    for copy in first:
        copy.wait()
    lane48 = lax.broadcasted_iota(jnp.int32, (48, 128), 1)
    second = []
    for group in range(GROUPS):
        for pair in range(2):
            stacked, local = [], []
            for b in (4 * group + 2 * pair, 4 * group + 2 * pair + 1):
                planes = [got[pl.ds(t * PLANES + b, 48, stride=36), :] for t in range(3)]
                planes.append(unpack_fourth(lane48, *planes))
                stacked.append(jnp.concatenate(planes, axis=0))
                offset = b * NG % 128
                start = b * NG - offset
                if offset + NG > 128:
                    part = pltpu.roll(potential_ref[:, start : start + 256], 256 - offset, 1)[:, :128]
                else:
                    part = potential_ref[:, start : start + 128]
                    if offset:
                        part = pltpu.roll(part, 128 - offset, 1)
                local.append(part)
            local = jnp.concatenate(local, axis=1)
            field = left_transform(left_ref, 1, jnp.concatenate(stacked, axis=1))
            field = jnp.concatenate([local, local], axis=0) * field
            field = left_transform(left_ref, 2, field)
            for column in range(2):
                planes = [field[48 * t : 48 * t + 48, 128 * column : 128 * column + 128] for t in range(4)]
                for t in range(3):
                    at = pl.ds(group * GROUP_ROWS + t * 4 + 2 * pair + column, 48, stride=PLANES)
                    back[at, :] = pack_fourth(lane48, planes[t], planes[3], t)
        second += start_group(1, group, back, fin)
    for copy in second + small:
        copy.wait()
    lane96 = lax.broadcasted_iota(jnp.int32, (NG, 128), 1)
    for g in range(GROUPS):
        parts = []
        for p in range(2):
            planes = [
                jnp.concatenate(
                    [
                        fin[pl.ds(g * 24 + p * PLANES + t * 4 + b, 24, stride=SENT), :]
                        for b in range(4)
                    ],
                    axis=0,
                )
                for t in range(3)
            ]
            planes.append(unpack_fourth(lane96, *planes))
            parts.append(planes)
        for pair in range(2):
            stacked = [
                jnp.concatenate([parts[0][t], parts[1][t]], axis=0) for t in (2 * pair, 2 * pair + 1)
            ]
            both = left_transform(left_ref, 3, jnp.concatenate(stacked, axis=1))
            for column in range(2):
                plane = both[:, 128 * column : 128 * column + 128]
                field = jnp.concatenate([plane[:NG], plane[NG:]], axis=1)
                field = right_transform(right_ref, 1, field)
                at = pl.ds((4 * g + 2 * pair + column) * NG, NG)
                out_real[at, :] = field[:, :128]
                out_imag[at, :] = field[:, 128:]


def pick_kernel(back_real, back_imag, leave_ref, wave_ref, index_ref, applied_ref, vr, vi):
    lane = lax.broadcasted_iota(jnp.int32, (BLOCK, 128), 1)
    for ref, source in ((vr, back_real), (vi, back_imag)):
        ref[pl.ds(0, GRID_ROWS), :] = source[...]
        ref[pl.ds(GRID_ROWS, GUARD), :] = jnp.zeros((GUARD, 128), jnp.float32)
    for bit in range(17):
        shift = 1 << bit
        needed = PACKED + sum(1 << k for k in range(bit + 1, 17)) // 128 + 1
        for step in range(GRID_ROWS // BLOCK):
            base = step * BLOCK
            if base >= needed:
                continue
            here = pl.ds(base, BLOCK)
            there = pl.ds(base + max(shift // 128, 1), BLOCK)
            arrives = (leave_ref[here, :] & shift) != 0
            for ref in (vr, vi):
                own, other = ref[here, :], ref[there, :]
                if shift < 128:
                    other = pltpu.roll(jnp.where(lane >= shift, own, other), 128 - shift, 1)
                ref[here, :] = jnp.where(arrives, other, own)

    def signed_square(position):
        signed = jnp.where(position < NG // 2, position, position - NG).astype(jnp.float32)
        return signed * signed

    for step in range(PACKED // BLOCK):
        base = step * BLOCK
        line, z = cell_of(index_ref[pl.ds(base, BLOCK), :])
        x, y = cell_of(line)
        energy = 2.0 * (signed_square(x) + signed_square(y) + signed_square(z)) / float((NG // 2) ** 2)
        for part, ref in enumerate((vr, vi)):
            at = pl.ds(2 * base + part, BLOCK, stride=2)
            applied_ref[at, :] = energy * wave_ref[at, :] + ref[pl.ds(base, BLOCK), :]


def rotate_kernel(
    applied_ref, rotations, order_ref, out_ref,
    window, mixed, send_sem, recv_sem, pair_send, pair_recv, out_send, out_recv, own_sem,
):
    band = lax.axis_index("band")
    chip, core = band // 2, band % 2
    sibling = {"band": chip * 2 + 1 - core}
    peers = [lax.rem(chip + turn, CHIPS) for turn in range(CHIPS)]
    barrier = pltpu.get_barrier_semaphore()
    pl.semaphore_signal(barrier, inc=1, device_id=sibling, device_id_type=MESH)
    for peer in peers[1:]:
        pl.semaphore_signal(barrier, inc=1, device_id={"band": peer * 2 + core}, device_id_type=MESH)
    pl.semaphore_wait(barrier, CHIPS)

    def inner(piece):
        return pl.ds(piece * PIECE, PIECE)

    def outer(which, piece):
        return pl.ds(pl.multiple_of(which * CHUNK + piece * PIECE, PIECE), PIECE)

    sent = []
    for piece in range(PIECES):
        row = []
        for turn, peer in enumerate(peers):
            source = applied_ref.at[outer(peer, piece), :]
            target = window.at[band, inner(piece), :]
            if turn:
                copy = pltpu.make_async_remote_copy(
                    src_ref=source,
                    dst_ref=target,
                    send_sem=send_sem.at[piece, turn],
                    recv_sem=recv_sem.at[piece, turn],
                    device_id={"band": peer * 2 + core},
                    device_id_type=MESH,
                )
            else:
                copy = pltpu.make_async_copy(source, target, own_sem.at[0, piece])
            copy.start()
            row.append(copy)
        sent.append(row)

    pairs, results = [], []
    for piece in range(PIECES):
        row = []
        for turn in range(CHIPS):
            if turn:
                sent[piece][turn].wait_recv()
            else:
                sent[piece][turn].wait()
            source = lax.rem(chip - turn + CHIPS, CHIPS) * 2 + core
            copy = pltpu.make_async_remote_copy(
                src_ref=window.at[source, inner(piece), :],
                dst_ref=window.at[source, inner(piece), :],
                send_sem=pair_send.at[piece, turn],
                recv_sem=pair_recv.at[piece, turn],
                device_id=sibling,
                device_id_type=MESH,
            )
            copy.start()
            row.append(copy)
        for copy in row:
            copy.wait_recv()
        pairs += row
        for turn in range(1, CHIPS + 1):
            peer = peers[turn % CHIPS]
            totals = [None] * OUT_LOCAL
            for i in range(BANDS):
                panel = order_ref[i]
                term = window[i, inner(piece), :]
                for j in range(OUT_LOCAL):
                    factor = rotations[panel // 2, panel % 2, (peer * 2 + core) * OUT_LOCAL + j]
                    totals[j] = factor * term if i == 0 else totals[j] + factor * term
            for j in range(OUT_LOCAL):
                mixed[turn - 1, j, inner(piece), :] = totals[j]
            source = mixed.at[turn - 1, :, inner(piece), :]
            target = out_ref.at[:, outer(chip, piece), :]
            if turn < CHIPS:
                copy = pltpu.make_async_remote_copy(
                    src_ref=source,
                    dst_ref=target,
                    send_sem=out_send.at[piece, turn],
                    recv_sem=out_recv.at[piece, turn],
                    device_id={"band": peer * 2 + core},
                    device_id_type=MESH,
                )
            else:
                copy = pltpu.make_async_copy(source, target, own_sem.at[1, piece])
            copy.start()
            results.append(copy)
    for row in sent:
        for copy in row[1:]:
            copy.wait_send()
    for copy in pairs:
        copy.wait_send()
    for copy in results:
        copy.wait()


def params(**more):
    return pltpu.CompilerParams(vmem_limit_bytes=VMEM_BYTES, **more)


def shards(wave_coeffs, potential, sphere_index, rotation, panel_order):
    f32 = jnp.float32
    bf16 = jnp.bfloat16
    values = wave_coeffs.astype(f32).reshape(2, PACKED, 128).transpose(1, 0, 2).reshape(2 * PACKED, 128)
    index = sphere_index.reshape(PACKED, 128)
    left, right = left_tables(), right_tables()
    grid_shape = jax.ShapeDtypeStruct((GRID_ROWS, 128), f32)
    exchange_buffer = pltpu.VMEM((GROUPS * GROUP_ROWS, 128), f32)
    dma = pltpu.SemaphoreType.DMA

    def wide(kind):
        return pltpu.VMEM((GUARD + GRID_ROWS, 128), kind)

    real, imag, leave = pl.pallas_call(
        spread_kernel,
        out_shape=(grid_shape, grid_shape, jax.ShapeDtypeStruct((GRID_ROWS, 128), jnp.int32)),
        in_specs=[VMEM_SPEC] * 2,
        out_specs=[VMEM_SPEC] * 3,
        scratch_shapes=[wide(f32), wide(f32), wide(jnp.int32)],
        compiler_params=params(),
        name="spread",
    )(index, values)
    real, imag, rotations = pl.pallas_call(
        fields_kernel,
        out_shape=(grid_shape, grid_shape, jax.ShapeDtypeStruct((PARTS, 2, 64), f32)),
        in_specs=[VMEM_SPEC, VMEM_SPEC, HBM_SPEC, VMEM_SPEC, HBM_SPEC, HBM_SPEC],
        out_specs=[VMEM_SPEC] * 3,
        scratch_shapes=[
            pltpu.VMEM(potential.shape, f32),
            pltpu.VMEM(left.shape, bf16),
            pltpu.VMEM(right.shape, bf16),
        ]
        + [exchange_buffer] * 4
        + [dma((2, GROUPS, PARTS)), dma((2, GROUPS, PARTS)), dma((2, GROUPS))]
        + [dma((PARTS,)), dma((PARTS,)), dma((4,))],
        compiler_params=params(collective_id=0, has_side_effects=True),
        name="fields",
    )(real, imag, potential, rotation, jnp.asarray(left), jnp.asarray(right))
    applied = pl.pallas_call(
        pick_kernel,
        out_shape=jax.ShapeDtypeStruct((2 * PACKED, 128), f32),
        in_specs=[VMEM_SPEC] * 5,
        out_specs=VMEM_SPEC,
        scratch_shapes=[wide(f32), wide(f32)],
        compiler_params=params(),
        name="pick",
    )(real, imag, leave, values, index)
    out = pl.pallas_call(
        rotate_kernel,
        out_shape=jax.ShapeDtypeStruct((OUT_LOCAL, 2 * PACKED, 128), f32),
        in_specs=[VMEM_SPEC, SMEM_SPEC, SMEM_SPEC],
        out_specs=VMEM_SPEC,
        scratch_shapes=[
            pltpu.VMEM((BANDS, CHUNK, 128), f32),
            pltpu.VMEM((CHIPS, OUT_LOCAL, CHUNK, 128), f32),
        ]
        + [dma((PIECES, CHIPS))] * 6
        + [dma((2, PIECES))],
        compiler_params=params(collective_id=1, has_side_effects=True),
        name="rotate",
    )(applied, rotations, panel_order)
    return out.reshape(OUT_LOCAL, PACKED, 2, 128).transpose(0, 2, 1, 3).reshape(OUT_LOCAL, 2, PACKED * 128)


def solution(mesh):
    return jax.shard_map(
        shards,
        mesh=mesh,
        in_specs=(P("band", None, "pw"), P(None, "pw"), P("pw"), P("pw", None), P()),
        out_specs=P("band", None, "pw"),
        check_vma=False,
    )
```

time: 1390 us -> 90.1 us (0.06)
  local copies, waits for them, and re-layouts: 644 us -> 6.08 us
  blocking collectives: 350 us -> 0 us
  other arithmetic: 279 us -> 1.11 us
  Pallas kernels: 0 us -> 82.5 us
  loops' own time: 36.7 us -> 0 us
  waiting for transfers between devices: 36.5 us -> 0 us
  starting transfers between devices: 18.2 us -> 0 us
    unnamed x1 -> x0, other arithmetic: 273 us -> none
    psum x16 -> x0, blocking collectives: 261 us -> none  [broadcast(): return lax.psum(block, axis)]
    gather x2 -> x0, local copies, waits for them, and re-layouts: 236 us -> none  [shards(): back = planes.reshape(band_count, 2, slab_cells)[:, :, local_index]]
    scatter x1 -> x0, local copies, waits for them, and re-layouts: 172 us -> none  [shards(): jnp.zeros((band_count, 2, slab_cells), jnp.float32).at[:, :, local_index]]
    all_to_all x1 -> x0, blocking collectives: 88.9 us -> none  [shards(): lax.all_to_all(combined, 'band', split_axis=0, concat_axis=2, tiled=True)]
    pallas_call x0 -> x4, Pallas kernels: none -> 82.5 us  [the longest x1 39.1 us: shards(): pl.pallas_call(rotate_kernel, out_shape=jax.ShapeDtypeStruct((OUT_LOCAL,...]
    unnamed x14 -> x15, local copies, waits for them, and re-layouts: 85.9 us -> 6.08 us
    add x1 -> x0, local copies, waits for them, and re-layouts: 43.8 us -> none  [shards(): applied = kinetic_term[None, None] * values + back]
  transfers between devices with their start and end apart: 3 -> 0, of which waited for: 2 -> 0; matrix products, arithmetic and copies ran while one was open for 1% -> 0% of each run, Pallas kernels for 0% -> 0%
where the time goes in v2:
time: 90.1 us; the launch traced here: 89.8 us
  Pallas kernels  82.5 us (92%)
  local copies, waits for them, and re-layouts  6.08 us (7%)
  other arithmetic  1.11 us (1%)
    pallas_call x1, Pallas kernels, shards(): pl.pallas_call(rotate_kernel, out_shape=jax.ShapeDtypeStruct((OUT_LOCAL,...  39.1 us
    pallas_call x1, Pallas kernels, shards(): pl.pallas_call(fields_kernel, out_shape=(grid_shape, grid_shape, jax.Shap...  33.1 us
    unnamed x15, local copies, waits for them, and re-layouts  6.08 us
    pallas_call x1, Pallas kernels, shards(): pl.pallas_call(spread_kernel, out_shape=(grid_shape, grid_shape, jax.Shap...  6.06 us
    pallas_call x1, Pallas kernels, shards(): pl.pallas_call(pick_kernel, out_shape=jax.ShapeDtypeStruct((2 * PACKED, 1...  4.22 us

profile of v2, /device:TPU:1, one launch (start us, length us, event | category | flops | bytes accessed | tf_op | source)
XLA Modules:
  0.0 89.8 jit_solution(4278135873044279654)
XLA Ops:
  0.0 1.1 %bitcast_convert_fusion = f32[2,480,128]{2,0,1:T(2,128)S(1)} fusion(bf16[1,2,61440]{2,1,0:T(2,128)(2,1)} %param.7), kind=kLoop, calls=%fused_computation | loop fusion | flops 122880 | bytes 737280 | tf_op jit(solution)/shard_map/reshape | solution.py:476
  1.1 0.0 copy-start
  1.1 0.9 %copy-done = s32[61440]{0:T(1024)S(1)} copy-done((s32[61440]{0:T(1024)S(1)}, s32[61440]{0:T(1024)}, u32[]{:S(2)}) %copy-start) | copy-done | bytes 245784
  2.1 0.0 copy-start.1
  2.1 6.1 %spread.1 = (f32[1152,128]{1,0:T(8,128)S(1)}, f32[1152,128]{1,0:T(8,128)S(1)}, s32[1152,128]{1,0:T(8,128)S(1)}) custom-call(s32[480,128]{1,0:T(8,128)S(1)} %bitcast.15, f32[960,128]{1,0:T(8,128)S(1)} %bitcast.13), custom_call_target="tpu_custom_call" | custom-call | tf_op jit(solution)/shard_map/spread/pallas_call | solution.py:486
  8.1 0.0 copy-start.2
  8.1 1.1 %copy-done.2 = bf16[4,2,192,192]{3,2,1,0:T(8,128)(2,1)S(1)} copy-done((bf16[4,2,192,192]{3,2,1,0:T(8,128)(2,1)S(1)}, bf16[4,2,192,192]{3,2,1,0:T(8,128)(2,1)}, u32[]{:S(2)}) %copy-start.2) | copy-done | bytes 589848
  9.3 0.0 copy-start.3
  9.3 1.0 %copy-done.3 = bf16[2,2,256,256]{3,2,1,0:T(8,128)(2,1)S(1)} copy-done((bf16[2,2,256,256]{3,2,1,0:T(8,128)(2,1)S(1)}, bf16[2,2,256,256]{3,2,1,0:T(8,128)(2,1)}, u32[]{:S(2)}) %copy-start.3) | copy-done | bytes 524312
  10.3 0.0 copy-start.4
  10.3 1.0 %copy-done.4 = f32[96,1152]{1,0:T(8,128)S(1)} copy-done((f32[96,1152]{1,0:T(8,128)S(1)}, f32[96,1152]{1,0:T(8,128)}, u32[]{:S(2)}) %copy-start.4) | copy-done | bytes 442392
  11.3 0.0 copy-start.5
  11.3 0.7 copy-done.5
  12.0 33.1 %fields.1 = (f32[1152,128]{1,0:T(8,128)S(1)}, f32[1152,128]{1,0:T(8,128)S(1)}, f32[8,2,64]{2,1,0:T(2,128)S(1)}) custom-call(f32[1152,128]{1,0:T(8,128)S(1)} %get-tuple-element.11.real_ref, f32[1152,128]{1,0:T(8,128)S(1)} %get-tuple-element.12.imag_ref, f32[96,1152]{1,0:T(8,128)S(1)} %copy-done.4, f32[2,64]{1,0:T(2,128)S(1)} %copy-done.5, ...), custom_call_target="tpu_custom_call" | custom-call | tf_op jit(solution)/shard_map/fields/pallas_call | solution.py:495
  45.1 0.0 copy-start.6
  45.1 0.0 copy-done.1
  45.2 4.2 %pick.1.applied_ref = f32[960,128]{1,0:T(8,128)S(1)} custom-call(f32[1152,128]{1,0:T(8,128)S(1)} %get-tuple-element.13.back_real, f32[1152,128]{1,0:T(8,128)S(1)} %get-tuple-element.14.back_imag, s32[1152,128]{1,0:T(8,128)S(1)} %get-tuple-element.15.leave_ref, f32[960,128]{1,0:T(8,128)S(1)} %bitcast.14, s32[480,128]{1,0:T(8,128)S(1)} %bitcast.16), custom_call_target="tpu_custom_call" | custom-call | tf_op jit(solution)/shard_map/pick/pallas_call | solution.py:511
  49.4 0.0 copy-done.6
  49.4 39.1 %rotate.1 = f32[4,960,128]{2,1,0:T(8,128)S(1)} custom-call(f32[960,128]{1,0:T(8,128)S(1)} %pick.1.applied_ref, f32[8,2,64]{2,1,0:T(2,128)S(1)} %get-tuple-element.16.rotations, s32[16]{0:T(128)S(1)} %copy-done.6), custom_call_target="tpu_custom_call" | custom-call | tf_op jit(solution)/shard_map/rotate/pallas_call | solution.py:520
  88.5 1.3 %copy.11 = f32[4,2,61440]{2,1,0:T(2,128)} copy(f32[4,2,61440]{2,1,0:T(2,128)S(1)} %bitcast.12) | data formatting | bytes 3932160
Async XLA Ops:
  1.1 0.9 %copy-start = (s32[61440]{0:T(1024)S(1)}, s32[61440]{0:T(1024)}, u32[]{:S(2)}) copy-start(s32[61440]{0:T(1024)} %param.9) | copy-start | bytes 737284
  2.1 43.1 %copy-start.1 = (s32[61440]{0:T(1024)S(1)}, s32[61440]{0:T(1024)}, u32[]{:S(2)}) copy-start(s32[61440]{0:T(1024)} %param.9) | copy-start | bytes 737284
  8.1 1.1 %copy-start.2 = (bf16[4,2,192,192]{3,2,1,0:T(8,128)(2,1)S(1)}, bf16[4,2,192,192]{3,2,1,0:T(8,128)(2,1)}, u32[]{:S(2)}) copy-start(bf16[4,2,192,192]{3,2,1,0:T(8,128)(2,1)} %constant.4.clone.left_hbm) | copy-start | bytes 1769476
  9.3 1.0 %copy-start.3 = (bf16[2,2,256,256]{3,2,1,0:T(8,128)(2,1)S(1)}, bf16[2,2,256,256]{3,2,1,0:T(8,128)(2,1)}, u32[]{:S(2)}) copy-start(bf16[2,2,256,256]{3,2,1,0:T(8,128)(2,1)} %constant.5.clone.right_hbm) | copy-start | bytes 1572868
  10.3 1.0 %copy-start.4 = (f32[96,1152]{1,0:T(8,128)S(1)}, f32[96,1152]{1,0:T(8,128)}, u32[]{:S(2)}) copy-start(f32[96,1152]{1,0:T(8,128)} %potential_hbm.1) | copy-start | bytes 1327108
  11.3 0.7 copy-start.5
  45.1 4.3 %copy-start.6 = (s32[16]{0:T(128)S(1)}, s32[16]{0:T(128)}, u32[]{:S(2)}) copy-start(s32[16]{0:T(128)} %order_ref.1) | copy-start | bytes 196

commit v3 on v2

--- a/solution.py
+++ b/solution.py
@@ -30,7 +30,7 @@
 VMEM_SPEC = pl.BlockSpec(memory_space=pltpu.VMEM)
 SMEM_SPEC = pl.BlockSpec(memory_space=pltpu.SMEM)
 HBM_SPEC = pl.BlockSpec(memory_space=pltpu.HBM)
-VMEM_BYTES = 48 * 1024 * 1024
+VMEM_BYTES = 60 * 1024 * 1024
 
 
 def split_table(table):
@@ -133,7 +133,7 @@
     )
 
 
-def spread_kernel(index_ref, wave_ref, real_ref, imag_ref, leave_ref, vr, vi, gap):
+def spread(index_ref, wave_ref, real_ref, imag_ref, leave_ref, vr, vi, gap, ready):
     first_line = lax.axis_index("pw") * GRID_ROWS
     lane = lax.broadcasted_iota(jnp.int32, (BLOCK, 128), 1)
     rows = lax.broadcasted_iota(jnp.int32, (BLOCK, 128), 0)
@@ -141,6 +141,7 @@
     for ref in (vr, vi):
         ref[pl.ds(0, GUARD), :] = jnp.zeros((GUARD, 128), jnp.float32)
         ref[pl.ds(GUARD + PACKED, GRID_ROWS - PACKED), :] = jnp.zeros((GRID_ROWS - PACKED, 128), jnp.float32)
+    ready()
     for step in range(PACKED // BLOCK):
         base = step * BLOCK
         line, z = cell_of(index_ref[pl.ds(base, BLOCK), :])
@@ -186,26 +187,13 @@
                 vi[here, :] = values[1]
 
 
-def fields_kernel(
-    real_ref, imag_ref, potential_hbm, rotation_ref, left_hbm, right_hbm,
-    out_real, out_imag, rotations,
+def fields(
+    real_ref, imag_ref, rotation_ref, out_real, out_imag, rotations,
     potential_ref, left_ref, right_ref, send, got, back, fin,
-    send_sem, recv_sem, own_sem, small_send, small_recv, load_sem,
+    send_sem, recv_sem, own_sem, small_send, small_recv, small_own, enter, tables_ready, potential_ready,
 ):
     me = lax.axis_index("pw")
     peers = [lax.rem(me + turn, PARTS) for turn in range(PARTS)]
-    loads = [
-        pltpu.make_async_copy(source, target, load_sem.at[k])
-        for k, (source, target) in enumerate(
-            ((right_hbm, right_ref), (left_hbm, left_ref), (potential_hbm, potential_ref))
-        )
-    ]
-    for load in loads:
-        load.start()
-    barrier = pltpu.get_barrier_semaphore()
-    for peer in peers[1:]:
-        pl.semaphore_signal(barrier, inc=1, device_id={"pw": peer}, device_id_type=MESH)
-
     def start_group(phase, group, source, target):
         copies = []
         for turn, peer in enumerate(peers):
@@ -228,8 +216,7 @@
             copies.append(copy)
         return copies
 
-    loads[0].wait()
-    loads[1].wait()
+    tables_ready()
     lane = lax.broadcasted_iota(jnp.int32, (2 * NG, 128), 1)
     first = []
     for g in range(GROUPS):
@@ -251,7 +238,7 @@
                     at = pl.ds(g * GROUP_ROWS + (p * 3 + t) * PLANES + b, PARTS, stride=SENT)
                     send[at, :] = packed[row : row + PARTS]
         if g == 0:
-            pl.semaphore_wait(barrier, PARTS - 1)
+            enter()
         first += start_group(0, g, send, got)
 
     small = []
@@ -266,11 +253,11 @@
                 device_id_type=MESH,
             )
         else:
-            copy = pltpu.make_async_copy(rotation_ref, rotations.at[me], load_sem.at[3])
+            copy = pltpu.make_async_copy(rotation_ref, rotations.at[me], small_own.at[0])
         copy.start()
         small.append(copy)
 
-    loads[2].wait()
+    potential_ready()
     for copy in first:
         copy.wait()
     lane48 = lax.broadcasted_iota(jnp.int32, (48, 128), 1)
@@ -333,11 +320,8 @@
                 out_imag[at, :] = field[:, 128:]
 
 
-def pick_kernel(back_real, back_imag, leave_ref, wave_ref, index_ref, applied_ref, vr, vi):
+def pick(leave_ref, wave_ref, index_ref, applied_ref, vr, vi):
     lane = lax.broadcasted_iota(jnp.int32, (BLOCK, 128), 1)
-    for ref, source in ((vr, back_real), (vi, back_imag)):
-        ref[pl.ds(0, GRID_ROWS), :] = source[...]
-        ref[pl.ds(GRID_ROWS, GUARD), :] = jnp.zeros((GUARD, 128), jnp.float32)
     for bit in range(17):
         shift = 1 << bit
         needed = PACKED + sum(1 << k for k in range(bit + 1, 17)) // 128 + 1
@@ -368,7 +352,7 @@
             applied_ref[at, :] = energy * wave_ref[at, :] + ref[pl.ds(base, BLOCK), :]
 
 
-def rotate_kernel(
+def rotate(
     applied_ref, rotations, order_ref, out_ref,
     window, mixed, send_sem, recv_sem, pair_send, pair_recv, out_send, out_recv, own_sem,
 ):
@@ -376,12 +360,6 @@
     chip, core = band // 2, band % 2
     sibling = {"band": chip * 2 + 1 - core}
     peers = [lax.rem(chip + turn, CHIPS) for turn in range(CHIPS)]
-    barrier = pltpu.get_barrier_semaphore()
-    pl.semaphore_signal(barrier, inc=1, device_id=sibling, device_id_type=MESH)
-    for peer in peers[1:]:
-        pl.semaphore_signal(barrier, inc=1, device_id={"band": peer * 2 + core}, device_id_type=MESH)
-    pl.semaphore_wait(barrier, CHIPS)
-
     def inner(piece):
         return pl.ds(piece * PIECE, PIECE)
 
@@ -466,8 +444,57 @@
         copy.wait()
 
 
-def params(**more):
-    return pltpu.CompilerParams(vmem_limit_bytes=VMEM_BYTES, **more)
+def whole_kernel(
+    index_hbm, wave_hbm, potential_hbm, rotation_ref, order_ref, left_hbm, right_hbm,
+    out_ref,
+    index_ref, wave_ref, potential_ref, left_ref, right_ref,
+    real_ref, imag_ref, leave_ref, vr, vi, gap, send, got, back, fin, rotations, factors, applied_ref, window, mixed,
+    load_sem, send_sem, recv_sem, own_sem, small_send, small_recv, small_own,
+    first_send, first_recv, pair_send, pair_recv, out_send, out_recv, band_own,
+):
+    loads = [
+        pltpu.make_async_copy(source, target, load_sem.at[k])
+        for k, (source, target) in enumerate((
+            (index_hbm, index_ref), (wave_hbm, wave_ref), (right_hbm, right_ref),
+            (left_hbm, left_ref), (potential_hbm, potential_ref),
+        ))
+    ]
+    for load in loads:
+        load.start()
+    me, band = lax.axis_index("pw"), lax.axis_index("band")
+    chip, core = band // 2, band % 2
+    barrier = pltpu.get_barrier_semaphore()
+    for turn in range(1, PARTS):
+        pl.semaphore_signal(
+            barrier, inc=1, device_id={"pw": lax.rem(me + turn, PARTS)}, device_id_type=MESH
+        )
+    for turn in range(1, CHIPS):
+        peer = lax.rem(chip + turn, CHIPS) * 2 + core
+        pl.semaphore_signal(barrier, inc=1, device_id={"band": peer}, device_id_type=MESH)
+    pl.semaphore_signal(barrier, inc=1, device_id={"band": chip * 2 + 1 - core}, device_id_type=MESH)
+
+    def ready(*which):
+        def wait():
+            for k in which:
+                loads[k].wait()
+
+        return wait
+
+    spread(index_ref, wave_ref, real_ref, imag_ref, leave_ref, vr, vi, gap, ready(0, 1))
+    fields(
+        real_ref, imag_ref, rotation_ref, vr, vi, rotations,
+        potential_ref, left_ref, right_ref, send, got, back, fin,
+        send_sem, recv_sem, own_sem, small_send, small_recv, small_own,
+        lambda: pl.semaphore_wait(barrier, PARTS - 1 + CHIPS), ready(2, 3), ready(4),
+    )
+    to_scalars = pltpu.make_async_copy(rotations, factors, small_own.at[1])
+    to_scalars.start()
+    pick(leave_ref, wave_ref, index_ref, applied_ref, vr, vi)
+    to_scalars.wait()
+    rotate(
+        applied_ref, factors, order_ref, out_ref, window, mixed,
+        first_send, first_recv, pair_send, pair_recv, out_send, out_recv, band_own,
+    )
 
 
 def shards(wave_coeffs, potential, sphere_index, rotation, panel_order):
@@ -476,61 +503,53 @@
     values = wave_coeffs.astype(f32).reshape(2, PACKED, 128).transpose(1, 0, 2).reshape(2 * PACKED, 128)
     index = sphere_index.reshape(PACKED, 128)
     left, right = left_tables(), right_tables()
-    grid_shape = jax.ShapeDtypeStruct((GRID_ROWS, 128), f32)
     exchange_buffer = pltpu.VMEM((GROUPS * GROUP_ROWS, 128), f32)
+    grid_buffer = pltpu.VMEM((GRID_ROWS, 128), f32)
     dma = pltpu.SemaphoreType.DMA
 
     def wide(kind):
         return pltpu.VMEM((GUARD + GRID_ROWS, 128), kind)
 
-    real, imag, leave = pl.pallas_call(
-        spread_kernel,
-        out_shape=(grid_shape, grid_shape, jax.ShapeDtypeStruct((GRID_ROWS, 128), jnp.int32)),
-        in_specs=[VMEM_SPEC] * 2,
-        out_specs=[VMEM_SPEC] * 3,
-        scratch_shapes=[wide(f32), wide(f32), wide(jnp.int32)],
-        compiler_params=params(),
-        name="spread",
-    )(index, values)
-    real, imag, rotations = pl.pallas_call(
-        fields_kernel,
-        out_shape=(grid_shape, grid_shape, jax.ShapeDtypeStruct((PARTS, 2, 64), f32)),
-        in_specs=[VMEM_SPEC, VMEM_SPEC, HBM_SPEC, VMEM_SPEC, HBM_SPEC, HBM_SPEC],
-        out_specs=[VMEM_SPEC] * 3,
+    out = pl.pallas_call(
+        whole_kernel,
+        out_shape=jax.ShapeDtypeStruct((OUT_LOCAL, 2 * PACKED, 128), f32),
+        in_specs=[HBM_SPEC, HBM_SPEC, HBM_SPEC, VMEM_SPEC, SMEM_SPEC, HBM_SPEC, HBM_SPEC],
+        out_specs=HBM_SPEC,
         scratch_shapes=[
+            pltpu.VMEM((PACKED, 128), jnp.int32),
+            pltpu.VMEM((2 * PACKED, 128), f32),
             pltpu.VMEM(potential.shape, f32),
             pltpu.VMEM(left.shape, bf16),
             pltpu.VMEM(right.shape, bf16),
+            grid_buffer,
+            grid_buffer,
+            pltpu.VMEM((GRID_ROWS, 128), jnp.int32),
+            wide(f32),
+            wide(f32),
+            wide(jnp.int32),
         ]
         + [exchange_buffer] * 4
-        + [dma((2, GROUPS, PARTS)), dma((2, GROUPS, PARTS)), dma((2, GROUPS))]
-        + [dma((PARTS,)), dma((PARTS,)), dma((4,))],
-        compiler_params=params(collective_id=0, has_side_effects=True),
-        name="fields",
-    )(real, imag, potential, rotation, jnp.asarray(left), jnp.asarray(right))
-    applied = pl.pallas_call(
-        pick_kernel,
-        out_shape=jax.ShapeDtypeStruct((2 * PACKED, 128), f32),
-        in_specs=[VMEM_SPEC] * 5,
-        out_specs=VMEM_SPEC,
-        scratch_shapes=[wide(f32), wide(f32)],
-        compiler_params=params(),
-        name="pick",
-    )(real, imag, leave, values, index)
-    out = pl.pallas_call(
-        rotate_kernel,
-        out_shape=jax.ShapeDtypeStruct((OUT_LOCAL, 2 * PACKED, 128), f32),
-        in_specs=[VMEM_SPEC, SMEM_SPEC, SMEM_SPEC],
-        out_specs=VMEM_SPEC,
-        scratch_shapes=[
+        + [
+            pltpu.VMEM((PARTS, 2, 64), f32),
+            pltpu.SMEM((PARTS, 2, 64), f32),
+            pltpu.VMEM((2 * PACKED, 128), f32),
             pltpu.VMEM((BANDS, CHUNK, 128), f32),
             pltpu.VMEM((CHIPS, OUT_LOCAL, CHUNK, 128), f32),
+            dma((5,)),
+            dma((2, GROUPS, PARTS)),
+            dma((2, GROUPS, PARTS)),
+            dma((2, GROUPS)),
+            dma((PARTS,)),
+            dma((PARTS,)),
+            dma((2,)),
         ]
         + [dma((PIECES, CHIPS))] * 6
         + [dma((2, PIECES))],
-        compiler_params=params(collective_id=1, has_side_effects=True),
-        name="rotate",
-    )(applied, rotations, panel_order)
+        compiler_params=pltpu.CompilerParams(
+            vmem_limit_bytes=VMEM_BYTES, collective_id=0, has_side_effects=True
+        ),
+        name="whole",
+    )(index, values, potential, rotation, panel_order, jnp.asarray(left), jnp.asarray(right))
     return out.reshape(OUT_LOCAL, PACKED, 2, 128).transpose(0, 2, 1, 3).reshape(OUT_LOCAL, 2, PACKED * 128)
 
 

time: 90.1 us -> 80.7 us (0.90)
  Pallas kernels: 82.5 us -> 75.6 us
  local copies, waits for them, and re-layouts: 6.08 us -> 2.94 us
    pallas_call x4 -> x1, Pallas kernels: 82.5 us -> 75.6 us  [shards(): pl.pallas_call(whole_kernel, out_shape=jax.ShapeDtypeStruct((OUT_LOCAL, 2...]
    unnamed x15 -> x1, local copies, waits for them, and re-layouts: 6.08 us -> 2.94 us
where the time goes in v3:
time: 80.7 us; the launch traced here: 80.5 us
  Pallas kernels  75.6 us (94%)
  local copies, waits for them, and re-layouts  2.94 us (4%)
  other arithmetic  1.89 us (2%)
    pallas_call x1, Pallas kernels, shards(): pl.pallas_call(whole_kernel, out_shape=jax.ShapeDtypeStruct((OUT_LOCAL, 2...  75.6 us
    unnamed x1, local copies, waits for them, and re-layouts  2.94 us
    reshape x1, other arithmetic, shards(): wave_coeffs.astype(f32).reshape(2, PACKED, 128).transpose(1, 0, 2)  1.89 us

profile of v3, /device:TPU:1, one launch (start us, length us, event | category | flops | bytes accessed | tf_op | source)
XLA Modules:
  0.0 80.5 jit_solution(12159209070234943073)
XLA Ops:
  0.0 1.9 %bitcast_convert_fusion = f32[2,480,128]{2,0,1:T(2,128)} fusion(bf16[1,2,61440]{2,1,0:T(2,128)(2,1)} %param.7), kind=kLoop, calls=%fused_computation | loop fusion | flops 122880 | bytes 737280 | tf_op jit(solution)/shard_map/reshape | solution.py:503
  1.9 75.6 %whole.1 = f32[4,960,128]{2,1,0:T(8,128)} custom-call(s32[480,128]{1,0:T(8,128)} %bitcast.14, f32[960,128]{1,0:T(8,128)} %bitcast.13, f32[96,1152]{1,0:T(8,128)} %potential_hbm.1, f32[2,64]{1,0:T(2,128)} %rotation_ref.1, s32[16]{0:T(128)} %order_ref.1, bf16[4,2,192,192]{3,2,1,0:T(8,128)(2,1)} %constant.4.clone.left_hbm, ...), custom_call_target="tpu_custom_call" | custom-call | tf_op jit(solution)/shard_map/whole/pallas_call | solution.py:513
  77.5 2.9 %copy.11 = f32[4,2,61440]{2,1,0:T(2,128)} copy(f32[4,2,61440]{2,1,0:T(2,128)} %bitcast.12) | data formatting | bytes 3932160

commit v4 on v3

--- a/solution.py
+++ b/solution.py
@@ -18,9 +18,11 @@
 GROUP_ROWS = PARTS * SENT
 PACKED = 480
 CHIPS = 8
-CHUNK = 2 * PACKED // CHIPS
-PIECES = 3
-PIECE = CHUNK // PIECES
+CUBE = ((4, (0, 1, 3, 2)), (1, (0, 3, 4, 7)), (3, (0, 1, 4, 5)))
+PIECES = len(CUBE)
+PARTED = 4
+CHUNK = 2 * PACKED // PIECES // PARTED
+HALF = CHUNK // 2
 BANDS = 16
 OUT_LOCAL = 4
 GUARD = 512
@@ -352,93 +354,102 @@
             applied_ref[at, :] = energy * wave_ref[at, :] + ref[pl.ds(base, BLOCK), :]
 
 
+def across(chip, mask):
+    z, x = chip // 4, chip % 4
+    x = (x, x + 1 - 2 * (x % 2), (x + 2) % 4, 3 - x)[mask % 4]
+    return (1 - z if mask >= 4 else z) * 4 + x
+
+
+def part_of(chip, piece):
+    z, x = chip // 4, chip % 4
+    near, far = (x + x // 2) % 2, x // 2
+    return (near + 2 * far, far + 2 * z, near + 2 * z)[piece]
+
+
 def rotate(
-    applied_ref, rotations, order_ref, out_ref,
-    window, mixed, send_sem, recv_sem, pair_send, pair_recv, out_send, out_recv, own_sem,
+    applied_ref, rotations, order_ref, out_ref, window, mixed,
+    first_send, first_recv, relay_send, relay_recv, out_send, out_recv, own_sem,
 ):
     band = lax.axis_index("band")
     chip, core = band // 2, band % 2
-    sibling = {"band": chip * 2 + 1 - core}
-    peers = [lax.rem(chip + turn, CHIPS) for turn in range(CHIPS)]
-    def inner(piece):
-        return pl.ds(piece * PIECE, PIECE)
-
-    def outer(which, piece):
-        return pl.ds(pl.multiple_of(which * CHUNK + piece * PIECE, PIECE), PIECE)
-
-    sent = []
-    for piece in range(PIECES):
-        row = []
-        for turn, peer in enumerate(peers):
-            source = applied_ref.at[outer(peer, piece), :]
-            target = window.at[band, inner(piece), :]
-            if turn:
-                copy = pltpu.make_async_remote_copy(
-                    src_ref=source,
-                    dst_ref=target,
-                    send_sem=send_sem.at[piece, turn],
-                    recv_sem=recv_sem.at[piece, turn],
-                    device_id={"band": peer * 2 + core},
-                    device_id_type=MESH,
-                )
-            else:
-                copy = pltpu.make_async_copy(source, target, own_sem.at[0, piece])
-            copy.start()
-            row.append(copy)
-        sent.append(row)
-
-    pairs, results = [], []
-    for piece in range(PIECES):
-        row = []
-        for turn in range(CHIPS):
-            if turn:
-                sent[piece][turn].wait_recv()
-            else:
-                sent[piece][turn].wait()
-            source = lax.rem(chip - turn + CHIPS, CHIPS) * 2 + core
+    cores = (core, 1 - core)
+
+    def rows(which, piece, half):
+        start = piece * PARTED * CHUNK + part_of(which, piece) * CHUNK + half * HALF
+        return pl.ds(pl.multiple_of(start, HALF), HALF)
+
+    def move(source, target, peer, turn, send, recv, own):
+        if turn:
             copy = pltpu.make_async_remote_copy(
-                src_ref=window.at[source, inner(piece), :],
-                dst_ref=window.at[source, inner(piece), :],
-                send_sem=pair_send.at[piece, turn],
-                recv_sem=pair_recv.at[piece, turn],
-                device_id=sibling,
+                src_ref=source,
+                dst_ref=target,
+                send_sem=send,
+                recv_sem=recv,
+                device_id={"band": peer},
                 device_id_type=MESH,
             )
-            copy.start()
-            row.append(copy)
-        for copy in row:
+        else:
+            copy = pltpu.make_async_copy(source, target, own)
+        copy.start()
+        return copy
+
+    sent, relayed, results = [], [], []
+    for piece, (_, masks) in enumerate(CUBE):
+        copies = []
+        for k, mask in enumerate(masks):
+            peer = across(chip, mask)
+            for c, half in enumerate(cores):
+                turn = 2 * k + c
+                copies.append(move(
+                    applied_ref.at[rows(peer, piece, half), :], window.at[piece, 2 * k + core],
+                    peer * 2 + half, turn, first_send.at[piece, turn], first_recv.at[piece, turn],
+                    own_sem.at[0, piece],
+                ))
+        sent.append(copies)
+
+    def relay(piece):
+        sent[piece][0].wait()
+        for copy in sent[piece][1:]:
             copy.wait_recv()
-        pairs += row
-        for turn in range(1, CHIPS + 1):
-            peer = peers[turn % CHIPS]
-            totals = [None] * OUT_LOCAL
-            for i in range(BANDS):
-                panel = order_ref[i]
-                term = window[i, inner(piece), :]
+        relayed.append(move(
+            window.at[piece, pl.ds(0, CHIPS)], window.at[piece, pl.ds(CHIPS, CHIPS)],
+            across(chip, CUBE[piece][0]) * 2 + core, 1, relay_send.at[piece], relay_recv.at[piece], None,
+        ))
+
+    def mix(piece):
+        shared, masks = CUBE[piece]
+        relayed[piece].wait_recv()
+        panels = []
+        for start in (chip, across(chip, shared)):
+            for mask in masks:
+                for c in range(2):
+                    panel = order_ref[across(start, mask) * 2 + c]
+                    panels.append((panel // 2, panel % 2))
+        for k in reversed(range(len(masks))):
+            for c in (1, 0):
+                peer = across(chip, masks[k]) * 2 + cores[c]
+                turn = 2 * k + c
+                totals = [None] * OUT_LOCAL
+                for i in range(BANDS):
+                    term = window[piece, i]
+                    for j in range(OUT_LOCAL):
+                        factor = rotations[panels[i][0], panels[i][1], peer * OUT_LOCAL + j]
+                        totals[j] = factor * term if i == 0 else totals[j] + factor * term
                 for j in range(OUT_LOCAL):
-                    factor = rotations[panel // 2, panel % 2, (peer * 2 + core) * OUT_LOCAL + j]
-                    totals[j] = factor * term if i == 0 else totals[j] + factor * term
-            for j in range(OUT_LOCAL):
-                mixed[turn - 1, j, inner(piece), :] = totals[j]
-            source = mixed.at[turn - 1, :, inner(piece), :]
-            target = out_ref.at[:, outer(chip, piece), :]
-            if turn < CHIPS:
-                copy = pltpu.make_async_remote_copy(
-                    src_ref=source,
-                    dst_ref=target,
-                    send_sem=out_send.at[piece, turn],
-                    recv_sem=out_recv.at[piece, turn],
-                    device_id={"band": peer * 2 + core},
-                    device_id_type=MESH,
-                )
-            else:
-                copy = pltpu.make_async_copy(source, target, own_sem.at[1, piece])
-            copy.start()
-            results.append(copy)
-    for row in sent:
-        for copy in row[1:]:
+                    mixed[piece, turn, j] = totals[j]
+                results.append(move(
+                    mixed.at[piece, turn], out_ref.at[:, rows(chip, piece, core), :],
+                    peer, turn, out_send.at[piece, turn], out_recv.at[piece, turn], own_sem.at[1, piece],
+                ))
+
+    for piece in range(PIECES):
+        relay(piece)
+    for piece in range(PIECES):
+        mix(piece)
+    for copies in sent:
+        for copy in copies[1:]:
             copy.wait_send()
-    for copy in pairs:
+    for copy in relayed:
         copy.wait_send()
     for copy in results:
         copy.wait()
@@ -447,31 +458,29 @@
 def whole_kernel(
     index_hbm, wave_hbm, potential_hbm, rotation_ref, order_ref, left_hbm, right_hbm,
     out_ref,
-    index_ref, wave_ref, potential_ref, left_ref, right_ref,
+    index_ref, narrow_ref, wave_ref, potential_ref, left_ref, right_ref,
     real_ref, imag_ref, leave_ref, vr, vi, gap, send, got, back, fin, rotations, factors, applied_ref, window, mixed,
     load_sem, send_sem, recv_sem, own_sem, small_send, small_recv, small_own,
-    first_send, first_recv, pair_send, pair_recv, out_send, out_recv, band_own,
+    first_send, first_recv, relay_send, relay_recv, out_send, out_recv, band_own,
 ):
     loads = [
         pltpu.make_async_copy(source, target, load_sem.at[k])
         for k, (source, target) in enumerate((
-            (index_hbm, index_ref), (wave_hbm, wave_ref), (right_hbm, right_ref),
+            (index_hbm, index_ref), (wave_hbm, narrow_ref), (right_hbm, right_ref),
             (left_hbm, left_ref), (potential_hbm, potential_ref),
         ))
     ]
     for load in loads:
         load.start()
     me, band = lax.axis_index("pw"), lax.axis_index("band")
-    chip, core = band // 2, band % 2
     barrier = pltpu.get_barrier_semaphore()
     for turn in range(1, PARTS):
         pl.semaphore_signal(
             barrier, inc=1, device_id={"pw": lax.rem(me + turn, PARTS)}, device_id_type=MESH
         )
-    for turn in range(1, CHIPS):
-        peer = lax.rem(chip + turn, CHIPS) * 2 + core
+    for turn in range(1, BANDS):
+        peer = lax.rem(band + turn, BANDS)
         pl.semaphore_signal(barrier, inc=1, device_id={"band": peer}, device_id_type=MESH)
-    pl.semaphore_signal(barrier, inc=1, device_id={"band": chip * 2 + 1 - core}, device_id_type=MESH)
 
     def ready(*which):
         def wait():
@@ -480,12 +489,16 @@
 
         return wait
 
-    spread(index_ref, wave_ref, real_ref, imag_ref, leave_ref, vr, vi, gap, ready(0, 1))
+    def inputs_ready():
+        ready(0, 1)()
+        wave_ref[...] = narrow_ref[...].astype(jnp.float32)
+
+    spread(index_ref, wave_ref, real_ref, imag_ref, leave_ref, vr, vi, gap, inputs_ready)
     fields(
         real_ref, imag_ref, rotation_ref, vr, vi, rotations,
         potential_ref, left_ref, right_ref, send, got, back, fin,
         send_sem, recv_sem, own_sem, small_send, small_recv, small_own,
-        lambda: pl.semaphore_wait(barrier, PARTS - 1 + CHIPS), ready(2, 3), ready(4),
+        lambda: pl.semaphore_wait(barrier, PARTS - 1 + BANDS - 1), ready(2, 3), ready(4),
     )
     to_scalars = pltpu.make_async_copy(rotations, factors, small_own.at[1])
     to_scalars.start()
@@ -493,14 +506,14 @@
     to_scalars.wait()
     rotate(
         applied_ref, factors, order_ref, out_ref, window, mixed,
-        first_send, first_recv, pair_send, pair_recv, out_send, out_recv, band_own,
+        first_send, first_recv, relay_send, relay_recv, out_send, out_recv, band_own,
     )
 
 
 def shards(wave_coeffs, potential, sphere_index, rotation, panel_order):
     f32 = jnp.float32
     bf16 = jnp.bfloat16
-    values = wave_coeffs.astype(f32).reshape(2, PACKED, 128).transpose(1, 0, 2).reshape(2 * PACKED, 128)
+    values = wave_coeffs.reshape(2, PACKED, 128).transpose(1, 0, 2).reshape(2 * PACKED, 128)
     index = sphere_index.reshape(PACKED, 128)
     left, right = left_tables(), right_tables()
     exchange_buffer = pltpu.VMEM((GROUPS * GROUP_ROWS, 128), f32)
@@ -517,6 +530,7 @@
         out_specs=HBM_SPEC,
         scratch_shapes=[
             pltpu.VMEM((PACKED, 128), jnp.int32),
+            pltpu.VMEM((2 * PACKED, 128), bf16),
             pltpu.VMEM((2 * PACKED, 128), f32),
             pltpu.VMEM(potential.shape, f32),
             pltpu.VMEM(left.shape, bf16),
@@ -533,8 +547,8 @@
             pltpu.VMEM((PARTS, 2, 64), f32),
             pltpu.SMEM((PARTS, 2, 64), f32),
             pltpu.VMEM((2 * PACKED, 128), f32),
-            pltpu.VMEM((BANDS, CHUNK, 128), f32),
-            pltpu.VMEM((CHIPS, OUT_LOCAL, CHUNK, 128), f32),
+            pltpu.VMEM((PIECES, BANDS, HALF, 128), f32),
+            pltpu.VMEM((PIECES, CHIPS, OUT_LOCAL, HALF, 128), f32),
             dma((5,)),
             dma((2, GROUPS, PARTS)),
             dma((2, GROUPS, PARTS)),
@@ -543,7 +557,9 @@
             dma((PARTS,)),
             dma((2,)),
         ]
-        + [dma((PIECES, CHIPS))] * 6
+        + [dma((PIECES, CHIPS))] * 2
+        + [dma((PIECES,))] * 2
+        + [dma((PIECES, CHIPS))] * 2
         + [dma((2, PIECES))],
         compiler_params=pltpu.CompilerParams(
             vmem_limit_bytes=VMEM_BYTES, collective_id=0, has_side_effects=True

time: 80.7 us -> 75.4 us (0.934)
  Pallas kernels: 75.6 us -> 72.2 us
  other arithmetic: 1.89 us -> 0 us
    pallas_call x1, Pallas kernels: 75.6 us -> 72.2 us  [shards(): pl.pallas_call(whole_kernel, out_shape=jax.ShapeDtypeStruct((OUT_LOCAL, 2...]
    reshape x1 -> x0, other arithmetic: 1.89 us -> none  [shards(): wave_coeffs.astype(f32).reshape(2, PACKED, 128).transpose(1, 0, 2)]
where the time goes in v4:
time: 75.4 us; the launch traced here: 75.2 us
  Pallas kernels  72.2 us (96%)
  local copies, waits for them, and re-layouts  2.94 us (4%)
    pallas_call x1, Pallas kernels, shards(): pl.pallas_call(whole_kernel, out_shape=jax.ShapeDtypeStruct((OUT_LOCAL, 2...  72.2 us
    unnamed x1, local copies, waits for them, and re-layouts  2.94 us

profile of v4, /device:TPU:1, one launch (start us, length us, event | category | flops | bytes accessed | tf_op | source)
XLA Modules:
  0.0 75.2 jit_solution(729668402138004343)
XLA Ops:
  0.0 72.2 %whole.1 = f32[4,960,128]{2,1,0:T(8,128)} custom-call(s32[480,128]{1,0:T(8,128)} %bitcast.12, bf16[960,128]{1,0:T(8,128)(2,1)} %bitcast.13, f32[96,1152]{1,0:T(8,128)} %potential_hbm.1, f32[2,64]{1,0:T(2,128)} %rotation_ref.1, s32[16]{0:T(128)} %order_ref.1, bf16[4,2,192,192]{3,2,1,0:T(8,128)(2,1)} %constant.4.clone.left_hbm, ...), custom_call_target="tpu_custom_call" | custom-call | tf_op jit(solution)/shard_map/whole/pallas_call | solution.py:526
  72.3 2.9 %copy.11 = f32[4,2,61440]{2,1,0:T(2,128)} copy(f32[4,2,61440]{2,1,0:T(2,128)} %bitcast.11) | data formatting | bytes 3932160

commit v5 on v4

--- a/solution.py
+++ b/solution.py
@@ -123,6 +123,10 @@
     return line, index - NG * line
 
 
+def along(value, lanes):
+    return jnp.take_along_axis(value, lanes, axis=1, mode="promise_in_bounds")
+
+
 def pack_fourth(lane, base, fourth, t):
     return jnp.where(lane < NG, base, pltpu.roll(fourth, NG - 32 * t, 1))
 
@@ -153,7 +157,7 @@
         vr[at, :] = wave_ref[pl.ds(2 * base, BLOCK, stride=2), :]
         vi[at, :] = wave_ref[pl.ds(2 * base + 1, BLOCK, stride=2), :]
 
-    for bit in range(16, -1, -1):
+    for bit in range(16, 6, -1):
         shift = 1 << bit
         reach = min(PACKED + sum(1 << k for k in range(bit, 17)) // 128 + 1, GRID_ROWS)
         for step in reversed(range(GRID_ROWS // BLOCK)):
@@ -164,29 +168,37 @@
                     leave_ref[leave_at, :] = jnp.zeros((BLOCK, 128), jnp.int32)
                 continue
             here = pl.ds(GUARD + base, BLOCK)
-            there = pl.ds(GUARD + base - max(shift // 128, 1), BLOCK)
+            there = pl.ds(GUARD + base - shift // 128, BLOCK)
             own = [ref[here, :] for ref in (gap, vr, vi)]
             other = [ref[there, :] for ref in (gap, vr, vi)]
-            if shift < 128:
-                stay = lane < 128 - shift
-                other = [pltpu.roll(jnp.where(stay, a, b), shift, 1) for a, b in zip(own, other)]
             arrives = (other[0] & shift) != 0
             leaves = own[0] & shift
-            left = jnp.where(leaves != 0, 0, own[0])
-            held = jnp.where(arrives, other[0], left)
-            if bit == 16:
-                leave_ref[leave_at, :] = leaves
-            else:
-                leave_ref[leave_at, :] = leave_ref[leave_at, :] | leaves
-            values = [jnp.where(arrives, other[k], own[k]) for k in (1, 2)]
-            if bit == 0:
-                filled = (held & FLAG) != 0
-                real_ref[leave_at, :] = jnp.where(filled, values[0], 0.0)
-                imag_ref[leave_at, :] = jnp.where(filled, values[1], 0.0)
-            else:
+            held = jnp.where(arrives, other[0], jnp.where(leaves != 0, 0, own[0]))
+            leaves = leaves if bit == 16 else leave_ref[leave_at, :] | leaves
+            leave_ref[leave_at, :] = leaves if bit > 7 else leaves | (held & 127)
+            gap[here, :] = held
+            for k, ref in ((1, vr), (2, vi)):
+                ref[here, :] = jnp.where(arrives, other[k], own[k])
+
+    for bit in range(6, -1, -1):
+        shift = 1 << bit
+        stay = lane < 128 - shift
+        for step in reversed(range(GRID_ROWS // BLOCK)):
+            here = pl.ds(GUARD + step * BLOCK, BLOCK)
+            before = pl.ds(GUARD + step * BLOCK - 1, BLOCK)
+            own = gap[here, :]
+            other = pltpu.roll(jnp.where(stay, own, gap[before, :]), shift, 1)
+            held = jnp.where((other & shift) != 0, other, jnp.where((own & shift) != 0, 0, own))
+            if bit:
                 gap[here, :] = held
-                vr[here, :] = values[0]
-                vi[here, :] = values[1]
+                continue
+            moved = held & 127
+            source = (lane - moved) & 127
+            filled = (held & FLAG) != 0
+            at = pl.ds(step * BLOCK, BLOCK)
+            for ref, target in ((vr, real_ref), (vi, imag_ref)):
+                value = jnp.where(lane >= moved, along(ref[here, :], source), along(ref[before, :], source))
+                target[at, :] = jnp.where(filled, value, 0.0)
 
 
 def fields(
@@ -324,7 +336,15 @@
 
 def pick(leave_ref, wave_ref, index_ref, applied_ref, vr, vi):
     lane = lax.broadcasted_iota(jnp.int32, (BLOCK, 128), 1)
-    for bit in range(17):
+    for step in range(GRID_ROWS // BLOCK):
+        here = pl.ds(step * BLOCK, BLOCK)
+        after = pl.ds(step * BLOCK + 1, BLOCK)
+        source = lane + (leave_ref[here, :] & 127)
+        inside = source < 128
+        source = source & 127
+        for ref in (vr, vi):
+            ref[here, :] = jnp.where(inside, along(ref[here, :], source), along(ref[after, :], source))
+    for bit in range(7, 17):
         shift = 1 << bit
         needed = PACKED + sum(1 << k for k in range(bit + 1, 17)) // 128 + 1
         for step in range(GRID_ROWS // BLOCK):
@@ -332,13 +352,10 @@
             if base >= needed:
                 continue
             here = pl.ds(base, BLOCK)
-            there = pl.ds(base + max(shift // 128, 1), BLOCK)
+            there = pl.ds(base + shift // 128, BLOCK)
             arrives = (leave_ref[here, :] & shift) != 0
             for ref in (vr, vi):
-                own, other = ref[here, :], ref[there, :]
-                if shift < 128:
-                    other = pltpu.roll(jnp.where(lane >= shift, own, other), 128 - shift, 1)
-                ref[here, :] = jnp.where(arrives, other, own)
+                ref[here, :] = jnp.where(arrives, ref[there, :], ref[here, :])
 
     def signed_square(position):
         signed = jnp.where(position < NG // 2, position, position - NG).astype(jnp.float32)
@@ -393,19 +410,18 @@
         copy.start()
         return copy
 
-    sent, relayed, results = [], [], []
-    for piece, (_, masks) in enumerate(CUBE):
-        copies = []
-        for k, mask in enumerate(masks):
-            peer = across(chip, mask)
+    relayed, results = [], []
+    sent = [[None] * CHIPS for _ in CUBE]
+    for k in reversed(range(PARTED)):
+        for piece, (_, masks) in enumerate(CUBE):
+            peer = across(chip, masks[k])
             for c, half in enumerate(cores):
                 turn = 2 * k + c
-                copies.append(move(
+                sent[piece][turn] = move(
                     applied_ref.at[rows(peer, piece, half), :], window.at[piece, 2 * k + core],
                     peer * 2 + half, turn, first_send.at[piece, turn], first_recv.at[piece, turn],
                     own_sem.at[0, piece],
-                ))
-        sent.append(copies)
+                )
 
     def relay(piece):
         sent[piece][0].wait()
@@ -416,36 +432,41 @@
             across(chip, CUBE[piece][0]) * 2 + core, 1, relay_send.at[piece], relay_recv.at[piece], None,
         ))
 
-    def mix(piece):
+    def panels_of(piece):
         shared, masks = CUBE[piece]
-        relayed[piece].wait_recv()
         panels = []
         for start in (chip, across(chip, shared)):
             for mask in masks:
                 for c in range(2):
                     panel = order_ref[across(start, mask) * 2 + c]
                     panels.append((panel // 2, panel % 2))
-        for k in reversed(range(len(masks))):
-            for c in (1, 0):
-                peer = across(chip, masks[k]) * 2 + cores[c]
-                turn = 2 * k + c
-                totals = [None] * OUT_LOCAL
-                for i in range(BANDS):
-                    term = window[piece, i]
-                    for j in range(OUT_LOCAL):
-                        factor = rotations[panels[i][0], panels[i][1], peer * OUT_LOCAL + j]
-                        totals[j] = factor * term if i == 0 else totals[j] + factor * term
-                for j in range(OUT_LOCAL):
-                    mixed[piece, turn, j] = totals[j]
-                results.append(move(
-                    mixed.at[piece, turn], out_ref.at[:, rows(chip, piece, core), :],
-                    peer, turn, out_send.at[piece, turn], out_recv.at[piece, turn], own_sem.at[1, piece],
-                ))
+        return panels
+
+    def mix(piece, k, c, panels):
+        peer = across(chip, CUBE[piece][1][k]) * 2 + cores[c]
+        turn = 2 * k + c
+        totals = [None] * OUT_LOCAL
+        for i in range(BANDS):
+            term = window[piece, i]
+            for j in range(OUT_LOCAL):
+                factor = rotations[panels[i][0], panels[i][1], peer * OUT_LOCAL + j]
+                totals[j] = factor * term if i == 0 else totals[j] + factor * term
+        for j in range(OUT_LOCAL):
+            mixed[piece, turn, j] = totals[j]
+        results.append(move(
+            mixed.at[piece, turn], out_ref.at[piece, part_of(chip, piece), core],
+            peer, turn, out_send.at[piece, turn], out_recv.at[piece, turn], own_sem.at[1, piece],
+        ))
 
     for piece in range(PIECES):
         relay(piece)
-    for piece in range(PIECES):
-        mix(piece)
+    panels = [panels_of(piece) for piece in range(PIECES)]
+    for k in reversed(range(PARTED)):
+        for piece in range(PIECES):
+            if k == PARTED - 1:
+                relayed[piece].wait_recv()
+            for c in (1, 0):
+                mix(piece, k, c, panels[piece])
     for copies in sent:
         for copy in copies[1:]:
             copy.wait_send()
@@ -525,7 +546,7 @@
 
     out = pl.pallas_call(
         whole_kernel,
-        out_shape=jax.ShapeDtypeStruct((OUT_LOCAL, 2 * PACKED, 128), f32),
+        out_shape=jax.ShapeDtypeStruct((PIECES, PARTED, 2, OUT_LOCAL, HALF, 128), f32),
         in_specs=[HBM_SPEC, HBM_SPEC, HBM_SPEC, VMEM_SPEC, SMEM_SPEC, HBM_SPEC, HBM_SPEC],
         out_specs=HBM_SPEC,
         scratch_shapes=[
@@ -566,6 +587,7 @@
         ),
         name="whole",
     )(index, values, potential, rotation, panel_order, jnp.asarray(left), jnp.asarray(right))
+    out = out.transpose(3, 0, 1, 2, 4, 5)
     return out.reshape(OUT_LOCAL, PACKED, 2, 128).transpose(0, 2, 1, 3).reshape(OUT_LOCAL, 2, PACKED * 128)
 
 

time: 75.4 us -> 73.8 us (0.979)
  Pallas kernels: 72.2 us -> 70.6 us
    transpose x0 -> x1, local copies, waits for them, and re-layouts: none -> 3.01 us  [shards(): out = out.transpose(3, 0, 1, 2, 4, 5)]
    unnamed x1 -> x0, local copies, waits for them, and re-layouts: 2.94 us -> none
    pallas_call x1, Pallas kernels: 72.2 us -> 70.6 us  [shards(): pl.pallas_call(whole_kernel, out_shape=jax.ShapeDtypeStruct((PIECES, PART...]
where the time goes in v5:
time: 73.8 us; the launch traced here: 73.6 us
  Pallas kernels  70.6 us (96%)
  local copies, waits for them, and re-layouts  3.01 us (4%)
    pallas_call x1, Pallas kernels, shards(): pl.pallas_call(whole_kernel, out_shape=jax.ShapeDtypeStruct((PIECES, PART...  70.6 us
    transpose x1, local copies, waits for them, and re-layouts, shards(): out = out.transpose(3, 0, 1, 2, 4, 5)  3.01 us

profile of v5, /device:TPU:1, one launch (start us, length us, event | category | flops | bytes accessed | tf_op | source)
XLA Modules:
  0.0 73.6 jit_solution(4827365889256913559)
XLA Ops:
  0.0 70.6 %whole.1 = f32[3,4,2,4,40,128]{5,4,3,2,1,0:T(8,128)} custom-call(s32[480,128]{1,0:T(8,128)} %bitcast.13, bf16[960,128]{1,0:T(8,128)(2,1)} %bitcast.14, f32[96,1152]{1,0:T(8,128)} %potential_hbm.1, f32[2,64]{1,0:T(2,128)} %rotation_ref.1, s32[16]{0:T(128)} %order_ref.1, bf16[4,2,192,192]{3,2,1,0:T(8,128)(2,1)} %constant.4.clone.left_hbm, ...), custom_call_target="tpu_custom_call" | custom-call | tf_op jit(solution)/shard_map/whole/pallas_call | solution.py:547
  70.6 3.0 %copy.10 = f32[4,3,4,2,40,128]{5,4,3,2,1,0:T(8,128)} copy(f32[4,3,4,2,40,128]{5,4,0,3,2,1:T(8,128)} %bitcast.12) | data formatting | bytes 3932160 | tf_op jit(solution)/shard_map/transpose | solution.py:590

commit v6 on v5

--- a/solution.py
+++ b/solution.py
@@ -361,7 +361,7 @@
         signed = jnp.where(position < NG // 2, position, position - NG).astype(jnp.float32)
         return signed * signed
 
-    for step in range(PACKED // BLOCK):
+    def finish(step):
         base = step * BLOCK
         line, z = cell_of(index_ref[pl.ds(base, BLOCK), :])
         x, y = cell_of(line)
@@ -370,6 +370,8 @@
             at = pl.ds(2 * base + part, BLOCK, stride=2)
             applied_ref[at, :] = energy * wave_ref[at, :] + ref[pl.ds(base, BLOCK), :]
 
+    return finish
+
 
 def across(chip, mask):
     z, x = chip // 4, chip % 4
@@ -384,7 +386,7 @@
 
 
 def rotate(
-    applied_ref, rotations, order_ref, out_ref, window, mixed,
+    finish, applied_ref, rotations, order_ref, out_ref, window, mixed,
     first_send, first_recv, relay_send, relay_recv, out_send, out_recv, own_sem,
 ):
     band = lax.axis_index("band")
@@ -412,8 +414,12 @@
 
     relayed, results = [], []
     sent = [[None] * CHIPS for _ in CUBE]
-    for k in reversed(range(PARTED)):
-        for piece, (_, masks) in enumerate(CUBE):
+    done = 0
+    for piece, (_, masks) in enumerate(CUBE):
+        while done * 2 * BLOCK < (piece + 1) * PARTED * CHUNK:
+            finish(done)
+            done += 1
+        for k in reversed(range(PARTED)):
             peer = across(chip, masks[k])
             for c, half in enumerate(cores):
                 turn = 2 * k + c
@@ -523,10 +529,10 @@
     )
     to_scalars = pltpu.make_async_copy(rotations, factors, small_own.at[1])
     to_scalars.start()
-    pick(leave_ref, wave_ref, index_ref, applied_ref, vr, vi)
+    finish = pick(leave_ref, wave_ref, index_ref, applied_ref, vr, vi)
     to_scalars.wait()
     rotate(
-        applied_ref, factors, order_ref, out_ref, window, mixed,
+        finish, applied_ref, factors, order_ref, out_ref, window, mixed,
         first_send, first_recv, relay_send, relay_recv, out_send, out_recv, band_own,
     )
 

time: 73.8 us -> 73.6 us (level)
  no operation moved by 1% of the time
where the time goes in v6:
time: 73.6 us; the launch traced here: 73.4 us
  Pallas kernels  70.4 us (96%)
  local copies, waits for them, and re-layouts  3.01 us (4%)
    pallas_call x1, Pallas kernels, shards(): pl.pallas_call(whole_kernel, out_shape=jax.ShapeDtypeStruct((PIECES, PART...  70.4 us
    transpose x1, local copies, waits for them, and re-layouts, shards(): out = out.transpose(3, 0, 1, 2, 4, 5)  3.01 us

profile of v6, /device:TPU:1, one launch (start us, length us, event | category | flops | bytes accessed | tf_op | source)
XLA Modules:
  0.0 73.4 jit_solution(9450950538571590852)
XLA Ops:
  0.0 70.4 %whole.1 = f32[3,4,2,4,40,128]{5,4,3,2,1,0:T(8,128)} custom-call(s32[480,128]{1,0:T(8,128)} %bitcast.13, bf16[960,128]{1,0:T(8,128)(2,1)} %bitcast.14, f32[96,1152]{1,0:T(8,128)} %potential_hbm.1, f32[2,64]{1,0:T(2,128)} %rotation_ref.1, s32[16]{0:T(128)} %order_ref.1, bf16[4,2,192,192]{3,2,1,0:T(8,128)(2,1)} %constant.4.clone.left_hbm, ...), custom_call_target="tpu_custom_call" | custom-call | tf_op jit(solution)/shard_map/whole/pallas_call | solution.py:553
  70.4 3.0 %copy.10 = f32[4,3,4,2,40,128]{5,4,3,2,1,0:T(8,128)} copy(f32[4,3,4,2,40,128]{5,4,0,3,2,1:T(8,128)} %bitcast.12) | data formatting | bytes 3932160 | tf_op jit(solution)/shard_map/transpose | solution.py:596

commit v7 on v6

--- a/solution.py
+++ b/solution.py
@@ -18,7 +18,7 @@
 GROUP_ROWS = PARTS * SENT
 PACKED = 480
 CHIPS = 8
-CUBE = ((4, (0, 1, 3, 2)), (1, (0, 3, 4, 7)), (3, (0, 1, 4, 5)))
+CUBE = ((4, (0, 1, 3, 2)), (1, (0, 3, 4, 7)), (3, (0, 4, 1, 5)))
 PIECES = len(CUBE)
 PARTED = 4
 CHUNK = 2 * PACKED // PIECES // PARTED
@@ -468,10 +468,10 @@
         relay(piece)
     panels = [panels_of(piece) for piece in range(PIECES)]
     for k in reversed(range(PARTED)):
-        for piece in range(PIECES):
-            if k == PARTED - 1:
-                relayed[piece].wait_recv()
-            for c in (1, 0):
+        for c in (1, 0):
+            for piece in range(PIECES):
+                if k == PARTED - 1 and c:
+                    relayed[piece].wait_recv()
                 mix(piece, k, c, panels[piece])
     for copies in sent:
         for copy in copies[1:]:

time: 73.6 us -> 73.3 us (level)
  no operation moved by 1% of the time
where the time goes in v7:
time: 73.3 us; the launch traced here: 73.1 us
  Pallas kernels  70.1 us (96%)
  local copies, waits for them, and re-layouts  3.01 us (4%)
    pallas_call x1, Pallas kernels, shards(): pl.pallas_call(whole_kernel, out_shape=jax.ShapeDtypeStruct((PIECES, PART...  70.1 us
    transpose x1, local copies, waits for them, and re-layouts, shards(): out = out.transpose(3, 0, 1, 2, 4, 5)  3.01 us

profile of v7, /device:TPU:1, one launch (start us, length us, event | category | flops | bytes accessed | tf_op | source)
XLA Modules:
  0.0 73.1 jit_solution(2548499168978882332)
XLA Ops:
  0.0 70.1 %whole.1 = f32[3,4,2,4,40,128]{5,4,3,2,1,0:T(8,128)} custom-call(s32[480,128]{1,0:T(8,128)} %bitcast.13, bf16[960,128]{1,0:T(8,128)(2,1)} %bitcast.14, f32[96,1152]{1,0:T(8,128)} %potential_hbm.1, f32[2,64]{1,0:T(2,128)} %rotation_ref.1, s32[16]{0:T(128)} %order_ref.1, bf16[4,2,192,192]{3,2,1,0:T(8,128)(2,1)} %constant.4.clone.left_hbm, ...), custom_call_target="tpu_custom_call" | custom-call | tf_op jit(solution)/shard_map/whole/pallas_call | solution.py:553
  70.1 3.0 %copy.10 = f32[4,3,4,2,40,128]{5,4,3,2,1,0:T(8,128)} copy(f32[4,3,4,2,40,128]{5,4,0,3,2,1:T(8,128)} %bitcast.12) | data formatting | bytes 3932160 | tf_op jit(solution)/shard_map/transpose | solution.py:596

commit v8 on v7

--- a/solution.py
+++ b/solution.py
@@ -419,9 +419,9 @@
         while done * 2 * BLOCK < (piece + 1) * PARTED * CHUNK:
             finish(done)
             done += 1
-        for k in reversed(range(PARTED)):
-            peer = across(chip, masks[k])
-            for c, half in enumerate(cores):
+        for c, half in ((1, cores[1]), (0, cores[0])):
+            for k in reversed(range(PARTED)):
+                peer = across(chip, masks[k])
                 turn = 2 * k + c
                 sent[piece][turn] = move(
                     applied_ref.at[rows(peer, piece, half), :], window.at[piece, 2 * k + core],

time: 73.3 us -> 72.2 us (0.985)
  Pallas kernels: 70.1 us -> 69.1 us
    pallas_call x1, Pallas kernels: 70.1 us -> 69.1 us  [shards(): pl.pallas_call(whole_kernel, out_shape=jax.ShapeDtypeStruct((PIECES, PART...]
where the time goes in v8:
time: 72.2 us; the launch traced here: 72.1 us
  Pallas kernels  69.1 us (96%)
  local copies, waits for them, and re-layouts  3.01 us (4%)
    pallas_call x1, Pallas kernels, shards(): pl.pallas_call(whole_kernel, out_shape=jax.ShapeDtypeStruct((PIECES, PART...  69.1 us
    transpose x1, local copies, waits for them, and re-layouts, shards(): out = out.transpose(3, 0, 1, 2, 4, 5)  3.01 us

profile of v8, /device:TPU:1, one launch (start us, length us, event | category | flops | bytes accessed | tf_op | source)
XLA Modules:
  0.0 72.1 jit_solution(15376422931207936606)
XLA Ops:
  0.0 69.1 %whole.1 = f32[3,4,2,4,40,128]{5,4,3,2,1,0:T(8,128)} custom-call(s32[480,128]{1,0:T(8,128)} %bitcast.13, bf16[960,128]{1,0:T(8,128)(2,1)} %bitcast.14, f32[96,1152]{1,0:T(8,128)} %potential_hbm.1, f32[2,64]{1,0:T(2,128)} %rotation_ref.1, s32[16]{0:T(128)} %order_ref.1, bf16[4,2,192,192]{3,2,1,0:T(8,128)(2,1)} %constant.4.clone.left_hbm, ...), custom_call_target="tpu_custom_call" | custom-call | tf_op jit(solution)/shard_map/whole/pallas_call | solution.py:553
  69.1 3.0 %copy.10 = f32[4,3,4,2,40,128]{5,4,3,2,1,0:T(8,128)} copy(f32[4,3,4,2,40,128]{5,4,0,3,2,1:T(8,128)} %bitcast.12) | data formatting | bytes 3932160 | tf_op jit(solution)/shard_map/transpose | solution.py:596
